TPU v7x, 32 devices: a whole 2x2x4 slice. The times are simulated.
32 devices in a mesh: ens: 2 (over y), mom: 8 (over z, x), src: 2 (over core).
Axes of the slice: x: 2, y: 2, z: 4, core: 2. Of those that a mesh axis runs over, the one named last changes fastest.
Arguments:
- fields: bfloat16 [16, 8, 2, 6, 2, 128, 128], P(('ens', 'mom'), 'src'), parts along dimension 0, may hold values from -0.29882812 to 0.29882812
- block_cols: int32 [16, 8, 6, 2], P(('ens', 'mom'), 'src'), parts along dimension 0, may hold values from 0 to 5, as said below
- sources: int32 [2], P('src'), may hold values from 0 to 7, as said below
- deltas: int32 [4], replicated, may hold values from 1 to 7
- partner: int32 [8], P('mom'), may hold values from 0 to 7, as said below
Outputs:
- correlator: float32 [2, 4, 16], P(None, 'src', ('ens', 'mom')), parts along dimension 2
There are 2 independent parts, one for each index of `ens`. A program takes and returns all parts, laid end to end along the dimension named above; an argument that names none is the same for every part. Nothing has to cross between parts.
Inputs may be any that keep to these rules, and one draw needn't show every extreme that they name: `block_cols`: within each block row of each field the 2 block columns are distinct. `sources`: entry s lies among the timeslices s * 4 to (s + 1) * 4 - 1. partner is an involution without fixed points. Momenta g * 1 to (g + 1) - 1 form group g; the partners of group g's momenta are the momenta of group g XOR (8 / 2).
All inputs are finite; a program needn't handle non-finite values.
Results may differ from a plain program's by a relative error of at most 0.0095.
Values may be sent and summed in bfloat16 or wider, within the bound.
No kernel may reach another device: no remote copies, remote signals or barrier semaphores. Data moves between devices by JAX's collectives and lax.ppermute only.
A program may use at most 128 MiB of HBM per device.

v0:
```python
import jax
import jax.numpy as jnp
from jax import lax
from jax.experimental import pallas as pl
from jax.experimental.pallas import tpu as pltpu
from jax.sharding import PartitionSpec as P

F32 = jnp.float32
BF16 = jnp.bfloat16
I32 = jnp.int32
SMEM = pl.BlockSpec(memory_space=pltpu.SMEM)
VMEM = pl.BlockSpec(memory_space=pltpu.VMEM)
ANY = pl.BlockSpec(memory_space=pl.ANY)


def one_way_pairs(count):
    half = count // 2
    outer = half // 2
    return [(g + half, g) if g < outer else (g, g + half) for g in range(half)]


def cost(flops, size):
    return pl.CostEstimate(flops=flops, bytes_accessed=size, transcendentals=0)


def pick_source_kernel(source_ref, fields_ref, out_ref, sems):
    time = lax.rem(source_ref[0], I32(fields_ref.shape[0]))
    copies = [
        pltpu.make_async_copy(fields_ref.at[time, part, r], out_ref.at[part, r], sems.at[part, r])
        for part in range(fields_ref.shape[1])
        for r in range(fields_ref.shape[2])
    ]
    for copy in copies:
        copy.start()
    for copy in copies:
        copy.wait()


def pick_source(source, fields):
    return pl.pallas_call(
        pick_source_kernel,
        out_shape=jax.ShapeDtypeStruct(fields.shape[1:], fields.dtype),
        in_specs=[SMEM, ANY],
        out_specs=VMEM,
        scratch_shapes=[pltpu.SemaphoreType.DMA(fields.shape[1:3])],
        cost_estimate=cost(0, 1_600_000),
        compiler_params=pltpu.CompilerParams(vmem_limit_bytes=52 * 2**20),
        name="pick_source",
    )(source, fields)


def pick_kernel(pieces, order_ref, fields_ref, *refs):
    *outs, sems = refs
    copies = [
        pltpu.make_async_copy(
            fields_ref.at[order_ref[slot], part, pl.ds(first, rows)], out.at[part], sems.at[at, part]
        )
        for at, ((slot, first, rows), out) in enumerate(zip(pieces, outs))
        for part in range(2)
    ]
    for copy in copies:
        copy.start()
    for copy in copies:
        copy.wait()


def pick_others(order, fields, pieces):
    return pl.pallas_call(
        lambda *refs: pick_kernel(pieces, *refs),
        out_shape=[
            jax.ShapeDtypeStruct((2, rows) + fields.shape[3:], fields.dtype) for _, _, rows in pieces
        ],
        in_specs=[SMEM, ANY],
        out_specs=[VMEM] * len(pieces),
        scratch_shapes=[pltpu.SemaphoreType.DMA((len(pieces), 2))],
        cost_estimate=cost(0, 5_000_000),
        compiler_params=pltpu.CompilerParams(vmem_limit_bytes=51 * 2**20),
        name="pick_others",
    )(order, fields)


def plan_kernel(core_ref, own_ref, other_ref, deltas_ref, order_ref, active_ref, full_ref, masks_ref):
    times = order_ref.shape[0]
    deltas = deltas_ref.shape[0]
    sinks = []
    for s, ref in enumerate((own_ref, other_ref)):
        for k in range(deltas):
            sinks.append(lax.rem(ref[0] + deltas_ref[k], I32(2 * times)))
    base = core_ref[0] * times
    first = own_ref[0] - base
    keys = []
    for t in range(times):
        needed = sinks[0] == base + t
        for sink in sinks[1:]:
            needed = needed | (sink == base + t)
        key = jnp.where(needed, I32(t), I32(times + t))
        keys.append(jnp.where(first == t, I32(-1), key))
    for t in range(times):
        rank = I32(0)
        for other in range(times):
            if other != t:
                rank += (keys[other] < keys[t]).astype(I32)
        order_ref[rank] = I32(t)
        for s in range(2):
            active = sinks[s * deltas] == base + t
            for k in range(1, deltas):
                active = active | (sinks[s * deltas + k] == base + t)
            active_ref[s * times + rank] = active.astype(I32)
    full = I32(0)
    for c in range(2):
        count = I32(0)
        for t in range(times):
            needed = (own_ref[0] == c * times + t) | (other_ref[0] == c * times + t)
            for sink in sinks:
                needed = needed | (sink == c * times + t)
            count += needed.astype(I32)
        full += jnp.where(count == times, I32(1 << c), I32(0))
    full_ref[0] = full
    for slot in range(times):
        time = base + order_ref[slot]
        for s in range(2):
            for k in range(deltas):
                own_first = sinks[s * deltas + (k + deltas // 2) % deltas]
                sink = jnp.where(core_ref[0] == 0, sinks[s * deltas + k], own_first)
                row = jnp.full((1, masks_ref.shape[2]), jnp.where(sink == time, F32(1), F32(0)))
                masks_ref[slot, s * deltas + k : s * deltas + k + 1] = row


def plan(core, own, other, deltas, times):
    return pl.pallas_call(
        plan_kernel,
        out_shape=[
            jax.ShapeDtypeStruct((times,), I32),
            jax.ShapeDtypeStruct((2 * times,), I32),
            jax.ShapeDtypeStruct((1,), I32),
            jax.ShapeDtypeStruct((times, 2 * deltas.shape[0], 128), F32),
        ],
        in_specs=[SMEM] * 4,
        out_specs=[SMEM] * 3 + [VMEM],
        cost_estimate=cost(0, 1000),
        name="plan",
    )(core, own, other, deltas)


def weights_kernel(s, pieces, order_ref, active_ref, *refs):
    far_ref, own_ref, far_cols, own_cols, m_cols, b_cols, a_ref, d_ref, *refs = refs
    *b_refs, u_ref, la, ld, bs, yn, held, sems = refs
    slot = pl.program_id(0)
    rows, per_row, size = a_ref.shape[1], a_ref.shape[2], a_ref.shape[3]
    times = order_ref.shape[0]
    step = rows * per_row
    base = order_ref[slot] * step
    a_base = lax.rem(far_ref[0], I32(times)) * step
    d_base = lax.rem(own_ref[0], I32(times)) * step
    lo, hi = pl.ds(0, size), pl.ds(size, size)

    b_copies = [[] for _ in range(times)]
    for at, ((piece_slot, first, count), b_ref) in enumerate(zip(pieces, b_refs)):
        for part in range(2):
            to = held.at[piece_slot % 2, part, pl.ds(first, count)]
            b_copies[piece_slot].append(pltpu.make_async_copy(b_ref.at[part], to, sems.at[at, part]))

    @pl.when(slot == 0)
    def _():
        for copy in b_copies[0]:
            copy.start()
        for r in range(rows):
            for j in range(per_row):
                real, imag = a_ref[0, r, j], a_ref[1, r, j]
                la[r, j, lo, lo] = real
                la[r, j, lo, hi] = -imag
                la[r, j, hi, lo] = imag
                la[r, j, hi, hi] = real
                real, imag = d_ref[0, r, j].T, d_ref[1, r, j].T
                ld[r, j, lo, lo] = real
                ld[r, j, lo, hi] = -imag
                ld[r, j, hi, lo] = imag
                ld[r, j, hi, hi] = real

    for at in range(times):

        @pl.when(slot == at)
        def _():
            for copy in b_copies[at + 1] if at + 1 < times else []:
                copy.start()
            for copy in b_copies[at]:
                copy.wait()

    @pl.when(active_ref[s * times + slot] == 0)
    def _():
        u_ref[...] = jnp.zeros_like(u_ref)

    @pl.when(active_ref[s * times + slot] != 0)
    def _():
        for r in range(rows):
            for j in range(per_row):
                bs[r, lo, pl.ds(j * size, size)] = held[slot % 2, 0, r, j]
                bs[r, hi, pl.ds(j * size, size)] = held[slot % 2, 1, r, j]

        yn[...] = jnp.zeros_like(yn)
        for r in range(rows):
            inners = [far_cols[a_base + r * per_row + j] for j in range(per_row)]
            parts = [
                jnp.dot(la[r, j], bs[inners[j]], preferred_element_type=F32) for j in range(per_row)
            ]
            pieces = []
            for j in range(per_row):
                for k in range(per_row):
                    col = b_cols[base + inners[j] * per_row + k]
                    pieces.append((j, col, parts[j][:, k * size : (k + 1) * size]))
            for at in reversed(range(len(pieces))):
                j, col, value = pieces[at]
                for other_j, other_col, other in pieces:
                    if other_j > j:
                        value = value + jnp.where(other_col == col, 1.0, 0.0) * other
                yn[col, pl.ds(r * size, size), lo] = value[:size].astype(BF16)
                yn[col, pl.ds(r * size, size), hi] = value[size:].astype(BF16)

        trace_real = jnp.zeros((size, size), F32)
        trace_imag = jnp.zeros((size, size), F32)
        for r in range(rows):
            trace_real += yn[r, pl.ds(r * size, size), lo].astype(F32)
            trace_imag += yn[r, pl.ds(r * size, size), hi].astype(F32)
        diagonal = lax.broadcasted_iota(I32, (size, size), 0) == lax.broadcasted_iota(I32, (size, size), 1)
        trace_real = jnp.sum(jnp.where(diagonal, trace_real, 0.0), axis=(0, 1), keepdims=True)
        trace_imag = jnp.sum(jnp.where(diagonal, trace_imag, 0.0), axis=(0, 1), keepdims=True)

        for r in range(rows):
            for j in range(per_row):
                col = m_cols[base + r * per_row + j]
                pick = I32(0)
                keep = F32(0)
                for k in range(per_row):
                    hit = own_cols[d_base + col * per_row + k] == r
                    pick = jnp.where(hit, I32(k), pick)
                    keep = jnp.where(hit, F32(1), keep)
                real = ld[col, pick, lo, lo].astype(F32)
                imag = ld[col, pick, hi, lo].astype(F32)
                weight_real, weight_imag = trace_real * keep, trace_imag * keep
                u_ref[0, r, j, 0] = weight_real * real - weight_imag * imag
                u_ref[0, r, j, 1] = weight_real * imag + weight_imag * real

        for i in range(rows):
            for j in range(per_row):
                r = own_cols[d_base + i * per_row + j]
                met = [m_cols[base + r * per_row + k] for k in range(per_row)]
                right = jnp.concatenate(
                    [yn[i, pl.ds(pl.multiple_of(col * size, size), size)] for col in met], axis=0
                )
                part = lax.dot_general(
                    ld[i, j], right, (((1,), (1,)), ((), ())), preferred_element_type=F32
                )
                for k in range(per_row):
                    u_ref[0, r, k, 0] -= part[:size, k * size : (k + 1) * size]
                    u_ref[0, r, k, 1] -= part[size:, k * size : (k + 1) * size]


def weights(flops, s, pieces, order, active, far_time, own_time, far_cols, own_cols, m_cols, b_cols, a, d, picked):
    times = order.shape[0]
    _, rows, per_row, size, _ = a.shape
    whole = lambda slot, *_: (0, 0, 0, 0, 0)
    return pl.pallas_call(
        lambda *refs: weights_kernel(s, pieces, *refs),
        out_shape=jax.ShapeDtypeStruct((times, rows, per_row, 2, size, size), F32),
        grid_spec=pltpu.PrefetchScalarGridSpec(
            num_scalar_prefetch=8,
            grid=(times,),
            in_specs=[
                pl.BlockSpec(a.shape, whole),
                pl.BlockSpec(a.shape, whole),
                *[ANY] * len(picked),
            ],
            out_specs=pl.BlockSpec(
                (1, rows, per_row, 2, size, size), lambda slot, *_: (slot, 0, 0, 0, 0, 0)
            ),
            scratch_shapes=[
                pltpu.VMEM((rows, per_row, 2 * size, 2 * size), BF16),
                pltpu.VMEM((rows, per_row, 2 * size, 2 * size), BF16),
                pltpu.VMEM((rows, 2 * size, per_row * size), BF16),
                pltpu.VMEM((rows, rows * size, 2 * size), BF16),
                pltpu.VMEM((2,) + a.shape, a.dtype),
                pltpu.SemaphoreType.DMA((len(picked), 2)),
            ],
        ),
        compiler_params=pltpu.CompilerParams(vmem_limit_bytes=24 * 2**20),
        cost_estimate=cost(flops, times * 1_000_000),
        name="weights",
    )(order, active, far_time, own_time, far_cols, own_cols, m_cols, b_cols, a, d, *picked)


def products(field_ref, u_refs, slot, first):
    _, rows, per_row, size, _ = field_ref.shape
    chunk = min(size, 32)
    fold = lambda x: jnp.sum(x.reshape(chunk // 8, 8, size), axis=0)
    sums = [jnp.zeros((8, size), F32) for _ in range(2 * len(u_refs))]
    for r in range(rows):
        for j in range(per_row):
            for start in range(0, size, chunk):
                at = pl.ds(start, chunk)
                real = field_ref[0, r, j, at].astype(F32)
                imag = field_ref[1, r, j, at].astype(F32)
                for s, u_ref in enumerate(u_refs):
                    u_real, u_imag = u_ref[slot, first + r, j, 0, at], u_ref[slot, first + r, j, 1, at]
                    sums[2 * s] += fold(real * u_real - imag * u_imag)
                    sums[2 * s + 1] += fold(real * u_imag + imag * u_real)
    return sums


def add_lines(slot, first, field_ref, u0_ref, u1_ref, masks_ref, before_ref):
    sums = products(field_ref, (u0_ref, u1_ref), slot, first)
    deltas = masks_ref.shape[1] // 2
    lines = []
    for part in range(2):
        for k in range(deltas):
            line = before_ref[part * deltas + k] if before_ref is not None else 0.0
            for s in range(2):
                at = s * deltas + k
                line = line + masks_ref[slot, at : at + 1] * sums[2 * s + part]
            lines.append(line)
    return lines


def inner_kernel(slot, first, field_ref, u0_ref, u1_ref, masks_ref, *refs):
    *before, out_ref = refs
    lines = add_lines(slot, first, field_ref, u0_ref, u1_ref, masks_ref, before[0] if before else None)
    for at, line in enumerate(lines):
        out_ref[at] = line


def inner(slot, first, field, u0, u1, masks, *before):
    return pl.pallas_call(
        lambda *refs: inner_kernel(slot, first, *refs),
        out_shape=jax.ShapeDtypeStruct((masks.shape[1], 8, field.shape[-1]), F32),
        in_specs=[VMEM] * (4 + len(before)),
        out_specs=VMEM,
        cost_estimate=cost(4_000_000, 4_000_000),
        compiler_params=pltpu.CompilerParams(vmem_limit_bytes=24 * 2**20),
        name="inner",
    )(field, u0, u1, masks, *before)


def stage_kernel(slot, u0_ref, u1_ref, masks_ref, out0_ref, out1_ref, out_masks_ref, sems, masks_sem):
    copies = [
        pltpu.make_async_copy(u_ref.at[slot, r], out_ref.at[0, r], sems.at[s, r])
        for s, (u_ref, out_ref) in enumerate(((u0_ref, out0_ref), (u1_ref, out1_ref)))
        for r in range(u_ref.shape[1])
    ]
    copies.append(pltpu.make_async_copy(masks_ref.at[slot], out_masks_ref.at[0], masks_sem))
    for copy in copies:
        copy.start()
    for copy in copies:
        copy.wait()


def stage(slot, u0, u1, masks):
    one = lambda value: jax.ShapeDtypeStruct((1,) + value.shape[1:], value.dtype)
    return pl.pallas_call(
        lambda *refs: stage_kernel(slot, *refs),
        out_shape=[one(u0), one(u1), one(masks)],
        in_specs=[ANY] * 3,
        out_specs=[VMEM] * 3,
        scratch_shapes=[pltpu.SemaphoreType.DMA((2, u0.shape[1])), pltpu.SemaphoreType.DMA],
        cost_estimate=cost(0, 6_000_000),
        compiler_params=pltpu.CompilerParams(vmem_limit_bytes=24 * 2**20),
        name="stage",
    )(u0, u1, masks)


def last_kernel(field_ref, u0_ref, u1_ref, masks_ref, before_ref, mine_ref, theirs_ref):
    lines = add_lines(0, 0, field_ref, u0_ref, u1_ref, masks_ref, before_ref)
    table = jnp.concatenate([jnp.sum(line, axis=0, keepdims=True) for line in lines], axis=0)
    table = jnp.sum(table, axis=1, keepdims=True)
    share = mine_ref.shape[1]
    for part in range(2):
        at = part * 2 * share
        mine_ref[part] = table[at : at + share]
        theirs_ref[part] = table[at + share : at + 2 * share]


def last(field, u0, u1, masks, lines):
    share = masks.shape[1] // 4
    return pl.pallas_call(
        last_kernel,
        out_shape=[jax.ShapeDtypeStruct((2, share, 1), F32)] * 2,
        in_specs=[VMEM] * 5,
        out_specs=[VMEM] * 2,
        cost_estimate=cost(4_000_000, 4_000_000),
        compiler_params=pltpu.CompilerParams(vmem_limit_bytes=24 * 2**20),
        name="last",
    )(field, u0, u1, masks, lines)


def local(fields, block_cols, sources, deltas, partner):
    assert fields.shape[0] == 1 and lax.axis_size("src") == 2
    del partner
    fields = fields[0]
    times = fields.shape[0]
    core = lax.axis_index("src").reshape(1)
    pairs = one_way_pairs(lax.axis_size("mom"))
    swap = lambda value: lax.ppermute(value, "src", [(0, 1), (1, 0)])
    to_partner = lambda value: lax.ppermute(value, "mom", pairs)

    cols = block_cols.reshape(-1)
    far_cols = to_partner(cols)
    own_field = pick_source(sources, fields)
    far = [to_partner(own_field)]

    other_time = swap(sources)
    order, active, full, masks = plan(core, sources, other_time, deltas, times)
    rows = fields.shape[2]
    half = rows // 2
    pieces = [(slot, 0, rows) for slot in range(times - 1)]
    pieces += [(times - 1, 0, half), (times - 1, half, rows - half)]
    picked = [own_field, *pick_others(order, fields, pieces[1:])]
    *early, near, late_low, late_high = picked
    far += [to_partner(field) for field in early[1:]]
    near, far[0] = lax.optimization_barrier((near, far[0]))
    near = to_partner(near)

    other_cols = swap(cols)
    far_other_cols = swap(far_cols)
    other_field = swap(own_field)
    far_other = swap(far[0])
    u0 = weights(
        80_000_000_000,
        0,
        pieces,
        order,
        active,
        sources,
        sources,
        far_cols,
        cols,
        far_cols,
        cols,
        far[0],
        own_field,
        picked,
    )
    u1 = weights(
        2_000_000_000,
        1,
        pieces,
        order,
        active,
        other_time,
        other_time,
        far_other_cols,
        other_cols,
        far_cols,
        cols,
        far_other,
        other_field,
        picked,
    )
    lines = inner(0, 0, far[0], u0, u1, masks)
    for slot, field in enumerate(far[1:], 1):
        lines = inner(slot, 0, field, u0, u1, masks, lines)

    both = ("mom", "src")

    def with_slot(cores):
        routes = [(2 * a + c, 2 * b + c) for a, b in pairs for c in cores]

        def branch(low, high, u0, u1, masks, lines):
            low, high = lax.ppermute(low, both, routes), lax.ppermute(high, both, routes)
            lines = inner(times - 1, 0, low, u0, u1, masks, lines)
            return inner(times - 1, half, high, u0, u1, masks, lines), *stage(times - 2, u0, u1, masks)

        return branch

    def without_slot(low, high, u0, u1, masks, lines):
        return lines, *stage(times - 2, u0, u1, masks)

    branches = [without_slot, with_slot([0]), with_slot([1]), with_slot([0, 1])]
    late_low, late_high, lines = lax.optimization_barrier((late_low, late_high, lines))
    lines, *staged = lax.switch(full[0], branches, late_low, late_high, u0, u1, masks, lines)
    mine, theirs = last(near, *staged, lines)

    total = mine + swap(theirs)
    back = [(2 * a + c, 2 * b + c) for b, a in pairs for c in range(2)]
    return total + lax.ppermute(total, both, back)


def solution(mesh):
    in_specs = (
        P(("ens", "mom"), "src", None, None, None, None, None),
        P(("ens", "mom"), "src", None, None),
        P("src"),
        P(),
        P("mom"),
    )
    out_specs = P(None, "src", ("ens", "mom"))
    return jax.shard_map(local, mesh=mesh, in_specs=in_specs, out_specs=out_specs, check_vma=False)
```

profile of v0, /device:TPU:8, one launch (start us, length us, event | category | flops | bytes accessed | tf_op | source)
XLA Modules:
  0.0 75.3 jit_solution(13930167616646825821)
XLA Ops:
  0.7 0.0 copy-start.2
  0.7 1.3 %pick_source.1.refs_9_.refs_10_ = bf16[2,6,2,128,128]{4,3,2,1,0:T(8,128)(2,1)S(1)} custom-call(s32[1]{0:T(128)S(6)} %copy.25.own_ref.source_ref.refs_2_.refs_3_, bf16[4,2,6,2,128,128]{5,4,3,2,1,0:T(8,128)(2,1)} %bitcast.3), custom_call_target="tpu_custom_call" | custom-call | bytes 1600000 | tf_op jit(solution)/shard_map/pick_source/pallas_call | solution.py:40
  1.9 4.5 %collective-permute-start.7 = (bf16[2,6,2,128,128]{4,3,2,1,0:T(8,128)(2,1)S(1)}, bf16[2,6,2,128,128]{4,3,2,1,0:T(8,128)(2,1)S(1)}, u32[]{:S(2)}, u32[]{:S(2)}) collective-permute-start(bf16[2,6,2,128,128]{4,3,2,1,0:T(8,128)(2,1)S(1)} %pick_source.1.refs_9_.refs_10_), channel_id=1, source_target_pairs={{8,0},{10,2},{4,12},{6,14},{9,1},{11,3},{5,13},{7,15},{24,16},{26,... | collective-permute-start | bytes 2359304 | tf_op jit(solution)/shard_map/ppermute | solution.py:401
  6.5 0.1 collective-permute-start.6
  6.6 0.0 copy-done.2
  6.6 0.1 copy.7
  6.7 0.1 reshape.10.refs_5_.refs_7_
  6.8 0.6 collective-permute-start.11
  7.3 1.3 %collective-permute-start.9 = (s32[48]{0:T(128)S(1)}, s32[48]{0:T(128)S(1)}, u32[]{:S(2)}, u32[]{:S(2)}) collective-permute-start(s32[48]{0:T(128)S(1)} %reshape.10.refs_5_.refs_7_), channel_id=1, source_target_pairs={{8,0},{10,2},{4,12},{6,14},{9,1},{11,3},{5,13},{7,15},{24,16},{26,... | collective-permute-start | bytes 584 | tf_op jit(solution)/shard_map/ppermute | solution.py:401
  8.6 0.1 collective-permute-start.13
  8.7 0.0 collective-permute-done.6.other_ref.refs_2_.refs_3_
  8.7 1.9 %plan.1 = (s32[4]{0:T(128)}, s32[8]{0:T(128)}, s32[1]{0:T(128)}, f32[4,8,128]{2,1,0:T(8,128)S(1)}) custom-call(s32[1]{0:T(128)} %bitcast.core_ref, s32[1]{0:T(128)S(6)} %copy.25.own_ref.source_ref.refs_2_.refs_3_, s32[1]{0:T(128)} %collective-permute-done.6.other_ref.refs_2_.refs_3_, s32[4]{0:T(128)} %deltas_ref.1), custom_call_target="tpu_custom_call" | custom-call | bytes 1000 | tf_op jit(solution)/shard_map/plan/pallas_call | solution.py:130
  10.6 0.0 copy-start
  10.7 0.6 copy-done
  11.3 0.0 copy-start.1
  11.3 2.2 %pick_others.1 = (bf16[2,6,2,128,128]{4,3,2,1,0:T(8,128)(2,1)S(1)}, bf16[2,6,2,128,128]{4,3,2,1,0:T(8,128)(2,1)S(1)}, bf16[2,3,2,128,128]{4,3,2,1,0:T(8,128)(2,1)S(1)}, bf16[2,3,2,128,128]{4,3,2,1,0:T(8,128)(2,1)S(1)}) custom-call(s32[4]{0:T(128)S(1)} %copy-done, bf16[4,2,6,2,128,128]{5,4,3,2,1,0:T(8,128)(2,1)} %bitcast.4), custom_call_target="tpu_custom_call" | custom-call | bytes 5000000 | tf_op jit(solution)/shard_map/pick_others/pallas_call | solution.py:68
  13.5 1.3 %collective-permute-start.14 = (bf16[2,6,2,128,128]{4,3,2,1,0:T(8,128)(2,1)S(1)}, bf16[2,6,2,128,128]{4,3,2,1,0:T(8,128)(2,1)S(1)}, u32[]{:S(2)}, u32[]{:S(2)}) collective-permute-start(bf16[2,6,2,128,128]{4,3,2,1,0:T(8,128)(2,1)S(1)} %get-tuple-element.108.refs_11_), channel_id=1, source_target_pairs={{8,0},{10,2},{4,12},{6,14},{9,1},{11,3},{5,13},{7,15},{24,16},{26,... | collective-permute-start | bytes 2359304 | tf_op jit(solution)/shard_map/ppermute | solution.py:401
  15.4 9.0 %collective-permute-done.9.refs_4_.refs_6_ = s32[48]{0:T(128)S(1)} collective-permute-done((s32[48]{0:T(128)S(1)}, s32[48]{0:T(128)S(1)}, u32[]{:S(2)}, u32[]{:S(2)}) %collective-permute-start.9) | collective-permute-done | bytes 224 | tf_op jit(solution)/shard_map/ppermute | solution.py:401
  24.4 0.0 collective-permute-start.10
  24.4 0.0 collective-permute-done.7.refs_8_.refs_0_
  24.4 6.2 %collective-permute-start.8 = (bf16[2,6,2,128,128]{4,3,2,1,0:T(8,128)(2,1)S(1)}, bf16[2,6,2,128,128]{4,3,2,1,0:T(8,128)(2,1)}, u32[]{:S(2)}, u32[]{:S(2)}) collective-permute-start(bf16[2,6,2,128,128]{4,3,2,1,0:T(8,128)(2,1)S(1)} %get-tuple-element.104.refs_12_), channel_id=1, source_target_pairs={{8,0},{10,2},{4,12},{6,14},{9,1},{11,3},{5,13},{7,15},{24,16},{26,... | collective-permute-start | bytes 2359304 | tf_op jit(solution)/shard_map/ppermute | solution.py:401
  30.6 0.0 collective-permute-done.11.refs_5_
  30.6 0.2 collective-permute-start.12
  30.8 0.0 copy-done.1
  30.8 8.0 %weights.2.refs_1_ = f32[4,6,2,2,128,128]{5,4,3,2,1,0:T(8,128)S(1)} custom-call(s32[4]{0:T(128)S(1)} %copy-done, s32[8]{0:T(128)S(1)} %copy-done.1, s32[1]{0:T(128)S(6)} %copy.25.own_ref.source_ref.refs_2_.refs_3_, s32[1]{0:T(128)S(6)} %copy.25.own_ref.source_ref.refs_2_.refs_3_, s32[48]{0:T(128)S(1)} %collective-permute-done.9.refs_4_.refs_6_, ...), custom_call_target="tpu_custom_call" | custom-call | flops 80000000000 | bytes 4000000 | tf_op jit(solution)/shard_map/weights/pallas_call | solution.py:262
  38.8 0.0 collective-permute-done.10.refs_4_
  38.8 0.0 collective-permute-done.13.refs_9_
  38.8 0.0 collective-permute-done.12.refs_8_
  38.8 9.3 %weights.3.refs_2_ = f32[4,6,2,2,128,128]{5,4,3,2,1,0:T(8,128)S(1)} custom-call(s32[4]{0:T(128)S(1)} %copy-done, s32[8]{0:T(128)S(1)} %copy-done.1, s32[1]{0:T(128)} %collective-permute-done.6.other_ref.refs_2_.refs_3_, s32[1]{0:T(128)} %collective-permute-done.6.other_ref.refs_2_.refs_3_, s32[48]{0:T(128)S(1)} %collective-permute-done.10.refs_4_, ...), custom_call_target="tpu_custom_call" | custom-call | flops 2000000000 | bytes 4000000 | tf_op jit(solution)/shard_map/weights/pallas_call | solution.py:262
  48.1 0.5 inner.14.refs_4_
  48.6 0.0 collective-permute-done.14.refs_0_
  48.6 0.5 inner.15
  49.2 2.4 %conditional.1 = (f32[8,8,128]{2,1,0:T(8,128)S(1)}, f32[1,6,2,2,128,128]{5,4,3,2,1,0:T(8,128)S(1)}, f32[1,6,2,2,128,128]{5,4,3,2,1,0:T(8,128)S(1)}, f32[1,8,128]{2,1,0:T(8,128)S(1)}) conditional(s32[]{:T(128)} %bitcast.2, (f32[4,6,2,2,128,128]{5,4,3,2,1,0:T(8,128)S(1)}, f32[4,6,2,2,128,128]{5,4,3,2,1,0:T(8,128)S(1)}, ...), branch_computations={%region_0.0_spmd, %region_1.0_spmd, %region_2.0_spmd, %region_3.0_... | conditional | flops 8000000 | bytes 17145840 | solution.py:477
  49.2 0.7 collective-permute-start.3
  49.9 0.7 collective-permute-start.2
  50.6 0.4 stage.6
  51.0 0.0 collective-permute-done.3.refs_0_
  51.0 0.3 inner.10.refs_4_
  51.2 0.0 collective-permute-done.2.refs_0_
  51.3 0.3 inner.11
  51.5 6.6 %collective-permute-done.8.field_ref = bf16[2,6,2,128,128]{4,3,2,1,0:T(8,128)(2,1)} collective-permute-done((bf16[2,6,2,128,128]{4,3,2,1,0:T(8,128)(2,1)S(1)}, bf16[2,6,2,128,128]{4,3,2,1,0:T(8,128)(2,1)}, u32[]{:S(2)}, u32[]{:S(2)}) %collective-permute-start.8) | collective-permute-done | bytes 786464 | tf_op jit(solution)/shard_map/ppermute | solution.py:401
  58.1 1.7 %last.1 = (f32[2,2,1]{2,1,0:T(2,128)S(1)}, f32[2,2,1]{2,1,0:T(2,128)S(1)}) custom-call(bf16[2,6,2,128,128]{4,3,2,1,0:T(8,128)(2,1)} %collective-permute-done.8.field_ref, f32[1,6,2,2,128,128]{5,4,3,2,1,0:T(8,128)S(1)} %get-tuple-element.115.u0_ref, f32[1,6,2,2,128,128]{5,4,3,2,1,0:T(8,128)S(1)} %get-tuple-element.116.u1_ref, ...), custom_call_target="tpu_custom_call" | custom-call | flops 4000000 | bytes 4000000 | tf_op jit(solution)/shard_map/last/pallas_call | solution.py:382
  59.8 7.7 %collective-permute-start.15 = (f32[2,2,1]{2,1,0:T(2,128)S(1)}, f32[2,2,1]{2,1,0:T(2,128)S(1)}, u32[]{:S(2)}, u32[]{:S(2)}) collective-permute-start(f32[2,2,1]{2,1,0:T(2,128)S(1)} %get-tuple-element.120), channel_id=1, source_target_pairs={{0,1},{1,0},{2,3},{3,2},{4,5},{5,4},{6,7},{7,6},{8,9},{9,8},{10,11... | collective-permute-start | bytes 56 | tf_op jit(solution)/shard_map/ppermute | solution.py:400
  67.5 0.8 %collective-permute-done.15 = f32[2,2,1]{2,1,0:T(2,128)S(1)} collective-permute-done((f32[2,2,1]{2,1,0:T(2,128)S(1)}, f32[2,2,1]{2,1,0:T(2,128)S(1)}, u32[]{:S(2)}, u32[]{:S(2)}) %collective-permute-start.15) | collective-permute-done | bytes 48 | tf_op jit(solution)/shard_map/ppermute | solution.py:400
  68.3 1.3 %collective-permute-start.16 = (f32[2,2,1]{2,1,0:T(2,128)S(1)}, f32[2,2,1]{2,1,0:T(2,128)S(1)}, u32[]{:S(2)}, u32[]{:S(2)}) collective-permute-start(f32[2,2,1]{2,1,0:T(2,128)S(1)} %add.6), channel_id=1, source_target_pairs={{0,8},{1,9},{2,10},{3,11},{12,4},{13,5},{14,6},{15,7},{16,24},{17,... | collective-permute-start | bytes 56 | tf_op jit(solution)/shard_map/ppermute | solution.py:482
  69.6 5.1 %collective-permute-done.16 = f32[2,2,1]{2,1,0:T(2,128)S(1)} collective-permute-done((f32[2,2,1]{2,1,0:T(2,128)S(1)}, f32[2,2,1]{2,1,0:T(2,128)S(1)}, u32[]{:S(2)}, u32[]{:S(2)}) %collective-permute-start.16) | collective-permute-done | bytes 48 | tf_op jit(solution)/shard_map/ppermute | solution.py:482
  74.7 0.7 copy.8
  (2 shorter events, 0.0 us)
Async XLA Ops:
  0.7 5.9 %copy-start.2 = (s32[1,4,6,2]{2,3,1,0:T(2,128)S(1)}, s32[1,4,6,2]{2,3,1,0:T(2,128)}, u32[]{:S(2)}) copy-start(s32[1,4,6,2]{2,3,1,0:T(2,128)} %param.10) | copy-start | bytes 580
  1.9 22.5 %collective-permute-start.7 = (bf16[2,6,2,128,128]{4,3,2,1,0:T(8,128)(2,1)S(1)}, bf16[2,6,2,128,128]{4,3,2,1,0:T(8,128)(2,1)S(1)}, u32[]{:S(2)}, u32[]{:S(2)}) collective-permute-start(bf16[2,6,2,128,128]{4,3,2,1,0:T(8,128)(2,1)S(1)} %pick_source.1.refs_9_.refs_10_), channel_id=1, source_target_pairs={{8,0},{10,2},{4,12},{6,14},{9,1},{11,3},{5,13},{7,15},{24,16},{26,... | collective-permute-start | bytes 2359304 | tf_op jit(solution)/shard_map/ppermute | solution.py:401
  6.5 2.2 %collective-permute-start.6 = (s32[1]{0:T(128)}, s32[1]{0:T(128)}, u32[]{:S(2)}, u32[]{:S(2)}) collective-permute-start(s32[1]{0:T(128)} %param.11), channel_id=1, source_target_pairs={{0,1},{1,0},{2,3},{3,2},{4,5},{5,4},{6,7},{7,6},{8,9},{9,8},{10,11... | collective-permute-start | bytes 20 | tf_op jit(solution)/shard_map/ppermute | solution.py:400
  6.8 23.8 %collective-permute-start.11 = (s32[48]{0:T(128)S(1)}, s32[48]{0:T(128)S(1)}, u32[]{:S(2)}, u32[]{:S(2)}) collective-permute-start(s32[48]{0:T(128)S(1)} %reshape.10.refs_5_.refs_7_), channel_id=1, source_target_pairs={{0,1},{1,0},{2,3},{3,2},{4,5},{5,4},{6,7},{7,6},{8,9},{9,8},{10,11... | collective-permute-start | bytes 584 | tf_op jit(solution)/shard_map/ppermute | solution.py:400
  7.3 17.1 %collective-permute-start.9 = (s32[48]{0:T(128)S(1)}, s32[48]{0:T(128)S(1)}, u32[]{:S(2)}, u32[]{:S(2)}) collective-permute-start(s32[48]{0:T(128)S(1)} %reshape.10.refs_5_.refs_7_), channel_id=1, source_target_pairs={{8,0},{10,2},{4,12},{6,14},{9,1},{11,3},{5,13},{7,15},{24,16},{26,... | collective-permute-start | bytes 584 | tf_op jit(solution)/shard_map/ppermute | solution.py:401
  8.6 30.2 %collective-permute-start.13 = (bf16[2,6,2,128,128]{4,3,2,1,0:T(8,128)(2,1)S(1)}, bf16[2,6,2,128,128]{4,3,2,1,0:T(8,128)(2,1)S(1)}, u32[]{:S(2)}, u32[]{:S(2)}) collective-permute-start(bf16[2,6,2,128,128]{4,3,2,1,0:T(8,128)(2,1)S(1)} %pick_source.1.refs_9_.refs_10_), channel_id=1, source_target_pairs={{0,1},{1,0},{2,3},{3,2},{4,5},{5,4},{6,7},{7,6},{8,9},{9,8},{10,11... | collective-permute-start | bytes 2359304 | tf_op jit(solution)/shard_map/ppermute | solution.py:400
  10.6 0.6 copy-start
  11.3 19.6 %copy-start.1 = (s32[8]{0:T(128)S(1)}, s32[8]{0:T(128)}, u32[]{:S(2)}) copy-start(s32[8]{0:T(128)} %get-tuple-element.106.refs_1_) | copy-start | bytes 100
  13.5 35.2 %collective-permute-start.14 = (bf16[2,6,2,128,128]{4,3,2,1,0:T(8,128)(2,1)S(1)}, bf16[2,6,2,128,128]{4,3,2,1,0:T(8,128)(2,1)S(1)}, u32[]{:S(2)}, u32[]{:S(2)}) collective-permute-start(bf16[2,6,2,128,128]{4,3,2,1,0:T(8,128)(2,1)S(1)} %get-tuple-element.108.refs_11_), channel_id=1, source_target_pairs={{8,0},{10,2},{4,12},{6,14},{9,1},{11,3},{5,13},{7,15},{24,16},{26,... | collective-permute-start | bytes 2359304 | tf_op jit(solution)/shard_map/ppermute | solution.py:401
  24.4 14.4 %collective-permute-start.10 = (s32[48]{0:T(128)S(1)}, s32[48]{0:T(128)S(1)}, u32[]{:S(2)}, u32[]{:S(2)}) collective-permute-start(s32[48]{0:T(128)S(1)} %collective-permute-done.9.refs_4_.refs_6_), channel_id=1, source_target_pairs={{0,1},{1,0},{2,3},{3,2},{4,5},{5,4},{6,7},{7,6},{8,9},{9,8},{10,11... | collective-permute-start | bytes 584 | tf_op jit(solution)/shard_map/ppermute | solution.py:400
  24.4 33.7 %collective-permute-start.8 = (bf16[2,6,2,128,128]{4,3,2,1,0:T(8,128)(2,1)S(1)}, bf16[2,6,2,128,128]{4,3,2,1,0:T(8,128)(2,1)}, u32[]{:S(2)}, u32[]{:S(2)}) collective-permute-start(bf16[2,6,2,128,128]{4,3,2,1,0:T(8,128)(2,1)S(1)} %get-tuple-element.104.refs_12_), channel_id=1, source_target_pairs={{8,0},{10,2},{4,12},{6,14},{9,1},{11,3},{5,13},{7,15},{24,16},{26,... | collective-permute-start | bytes 2359304 | tf_op jit(solution)/shard_map/ppermute | solution.py:401
  30.6 8.2 %collective-permute-start.12 = (bf16[2,6,2,128,128]{4,3,2,1,0:T(8,128)(2,1)S(1)}, bf16[2,6,2,128,128]{4,3,2,1,0:T(8,128)(2,1)S(1)}, u32[]{:S(2)}, u32[]{:S(2)}) collective-permute-start(bf16[2,6,2,128,128]{4,3,2,1,0:T(8,128)(2,1)S(1)} %collective-permute-done.7.refs_8_.refs_0_), channel_id=1, source_target_pairs={{0,1},{1,0},{2,3},{3,2},{4,5},{5,4},{6,7},{7,6},{8,9},{9,8},{10,11... | collective-permute-start | bytes 2359304 | tf_op jit(solution)/shard_map/ppermute | solution.py:400
  49.2 1.8 %collective-permute-start.3 = (bf16[2,3,2,128,128]{4,3,2,1,0:T(8,128)(2,1)S(1)}, bf16[2,3,2,128,128]{4,3,2,1,0:T(8,128)(2,1)S(1)}, u32[]{:S(2)}, u32[]{:S(2)}) collective-permute-start(bf16[2,3,2,128,128]{4,3,2,1,0:T(8,128)(2,1)S(1)} %get-tuple-element.69), channel_id=1, source_target_pairs={{9,1},{11,3},{5,13},{7,15},{25,17},{27,19},{21,29},{23,31}} | collective-permute-start | bytes 1179656 | tf_op jit(solution)/shard_map/cond/branch_2_fun/ppermute | solution.py:466
  49.9 1.4 %collective-permute-start.2 = (bf16[2,3,2,128,128]{4,3,2,1,0:T(8,128)(2,1)S(1)}, bf16[2,3,2,128,128]{4,3,2,1,0:T(8,128)(2,1)S(1)}, u32[]{:S(2)}, u32[]{:S(2)}) collective-permute-start(bf16[2,3,2,128,128]{4,3,2,1,0:T(8,128)(2,1)S(1)} %get-tuple-element.65), channel_id=1, source_target_pairs={{9,1},{11,3},{5,13},{7,15},{25,17},{27,19},{21,29},{23,31}} | collective-permute-start | bytes 1179656 | tf_op jit(solution)/shard_map/cond/branch_2_fun/ppermute | solution.py:466
  59.8 8.5 %collective-permute-start.15 = (f32[2,2,1]{2,1,0:T(2,128)S(1)}, f32[2,2,1]{2,1,0:T(2,128)S(1)}, u32[]{:S(2)}, u32[]{:S(2)}) collective-permute-start(f32[2,2,1]{2,1,0:T(2,128)S(1)} %get-tuple-element.120), channel_id=1, source_target_pairs={{0,1},{1,0},{2,3},{3,2},{4,5},{5,4},{6,7},{7,6},{8,9},{9,8},{10,11... | collective-permute-start | bytes 56 | tf_op jit(solution)/shard_map/ppermute | solution.py:400
  68.3 6.4 %collective-permute-start.16 = (f32[2,2,1]{2,1,0:T(2,128)S(1)}, f32[2,2,1]{2,1,0:T(2,128)S(1)}, u32[]{:S(2)}, u32[]{:S(2)}) collective-permute-start(f32[2,2,1]{2,1,0:T(2,128)S(1)} %add.6), channel_id=1, source_target_pairs={{0,8},{1,9},{2,10},{3,11},{12,4},{13,5},{14,6},{15,7},{16,24},{17,... | collective-permute-start | bytes 56 | tf_op jit(solution)/shard_map/ppermute | solution.py:482
where the time goes:
time: 75.9 us; the launch traced here: 75.3 us
  Pallas kernels  26.2 us (35%)
  starting transfers between devices  24.6 us (32%)
  waiting for transfers between devices  21.5 us (28%)
  local copies, waits for them, and re-layouts  1.49 us (2%)
  between operations  1.42 us (2%)
    pallas_call x2, Pallas kernels, weights(): pl.pallas_call(lambda *refs: weights_kernel(s, pieces, *refs), out_shape=...  17.2 us
    ppermute x4, waiting for transfers between devices, local(): to_partner = lambda value: lax.ppermute(value, 'mom', pairs)  15.5 us
    ppermute x4, starting transfers between devices, local(): to_partner = lambda value: lax.ppermute(value, 'mom', pairs)  13.4 us
    ppermute x6, starting transfers between devices, local(): swap = lambda value: lax.ppermute(value, 'src', [(0, 1), (1, 0)])  8.63 us
    ppermute x1, waiting for transfers between devices, local(): return total + lax.ppermute(total, both, back)  5.08 us
    pallas_call x1, Pallas kernels, pick_others(): pl.pallas_call(lambda *refs: pick_kernel(pieces, *refs), out_shape=[jax.S...  2.19 us
    pallas_call x1, Pallas kernels, plan(): pl.pallas_call(plan_kernel, out_shape=[jax.ShapeDtypeStruct((times,), I32...  1.91 us
    pallas_call x1, Pallas kernels, last(): pl.pallas_call(last_kernel, out_shape=[jax.ShapeDtypeStruct((2, share, 1)...  1.7 us
  transfers between devices with their start and end apart: 13, of which 4 were waited for; matrix products, arithmetic and copies ran while one was open for 0% of the time, Pallas kernels for 31%

commit v1 on v0

--- a/solution.py
+++ b/solution.py
@@ -282,7 +282,7 @@
                 pltpu.SemaphoreType.DMA((len(picked), 2)),
             ],
         ),
-        compiler_params=pltpu.CompilerParams(vmem_limit_bytes=24 * 2**20),
+        compiler_params=pltpu.CompilerParams(vmem_limit_bytes=16 * 2**20),
         cost_estimate=cost(flops, times * 1_000_000),
         name="weights",
     )(order, active, far_time, own_time, far_cols, own_cols, m_cols, b_cols, a, d, *picked)
@@ -334,7 +334,7 @@
         in_specs=[VMEM] * (4 + len(before)),
         out_specs=VMEM,
         cost_estimate=cost(4_000_000, 4_000_000),
-        compiler_params=pltpu.CompilerParams(vmem_limit_bytes=24 * 2**20),
+        compiler_params=pltpu.CompilerParams(vmem_limit_bytes=16 * 2**20),
         name="inner",
     )(field, u0, u1, masks, *before)
 
@@ -361,7 +361,7 @@
         out_specs=[VMEM] * 3,
         scratch_shapes=[pltpu.SemaphoreType.DMA((2, u0.shape[1])), pltpu.SemaphoreType.DMA],
         cost_estimate=cost(0, 6_000_000),
-        compiler_params=pltpu.CompilerParams(vmem_limit_bytes=24 * 2**20),
+        compiler_params=pltpu.CompilerParams(vmem_limit_bytes=8 * 2**20),
         name="stage",
     )(u0, u1, masks)
 
@@ -385,7 +385,7 @@
         in_specs=[VMEM] * 5,
         out_specs=[VMEM] * 2,
         cost_estimate=cost(4_000_000, 4_000_000),
-        compiler_params=pltpu.CompilerParams(vmem_limit_bytes=24 * 2**20),
+        compiler_params=pltpu.CompilerParams(vmem_limit_bytes=8 * 2**20),
         name="last",
     )(field, u0, u1, masks, lines)
 

time: 75.9 us -> 84.4 us (1.11)
  waiting for transfers between devices: 21.5 us -> 36.5 us
  starting transfers between devices: 24.6 us -> 18.2 us
    ppermute x1, waiting for transfers between devices: 0.01 us -> 14.3 us  [branch(): lax.ppermute(low, both, routes)]
    ppermute x6, starting transfers between devices: 8.63 us -> 0.95 us  [local(): swap = lambda value: lax.ppermute(value, 'src', [(0, 1), (1, 0)])]
    ppermute x1, waiting for transfers between devices: 0.01 us -> 7.01 us  [branch(): lax.ppermute(high, both, routes)]
    ppermute x4, waiting for transfers between devices: 15.5 us -> 9 us  [local(): to_partner = lambda value: lax.ppermute(value, 'mom', pairs)]
  transfers between devices with their start and end apart: 13 -> 13, of which waited for: 4 -> 5; matrix products, arithmetic and copies ran while one was open for 0% -> 0% of each run, Pallas kernels for 31% -> 28%
where the time goes in v1:
time: 84.4 us; the launch traced here: 84 us
  waiting for transfers between devices  36.5 us (43%)
  Pallas kernels  26.2 us (31%)
  starting transfers between devices  18.2 us (22%)
  local copies, waits for them, and re-layouts  1.49 us (2%)
  between operations  1.43 us (2%)
    pallas_call x2, Pallas kernels, weights(): pl.pallas_call(lambda *refs: weights_kernel(s, pieces, *refs), out_shape=...  17.2 us
    ppermute x1, waiting for transfers between devices, branch(): lax.ppermute(low, both, routes)  14.3 us
    ppermute x4, starting transfers between devices, local(): to_partner = lambda value: lax.ppermute(value, 'mom', pairs)  13.4 us
    ppermute x4, waiting for transfers between devices, local(): to_partner = lambda value: lax.ppermute(value, 'mom', pairs)  9 us
    ppermute x1, waiting for transfers between devices, branch(): lax.ppermute(high, both, routes)  7.01 us
    ppermute x1, waiting for transfers between devices, local(): return total + lax.ppermute(total, both, back)  5.08 us
    pallas_call x1, Pallas kernels, pick_others(): pl.pallas_call(lambda *refs: pick_kernel(pieces, *refs), out_shape=[jax.S...  2.19 us
    pallas_call x1, Pallas kernels, plan(): pl.pallas_call(plan_kernel, out_shape=[jax.ShapeDtypeStruct((times,), I32...  1.91 us
  transfers between devices with their start and end apart: 13, of which 5 were waited for; matrix products, arithmetic and copies ran while one was open for 0% of the time, Pallas kernels for 28%

profile of v1, /device:TPU:8, one launch (start us, length us, event | category | flops | bytes accessed | tf_op | source)
XLA Modules:
  0.0 84.0 jit_solution(1854179016447343209)
XLA Ops:
  0.7 0.0 copy-start.2
  0.7 1.3 %pick_source.1.refs_9_.refs_10_ = bf16[2,6,2,128,128]{4,3,2,1,0:T(8,128)(2,1)S(1)} custom-call(s32[1]{0:T(128)S(6)} %copy.25.own_ref.source_ref.refs_2_.refs_3_, bf16[4,2,6,2,128,128]{5,4,3,2,1,0:T(8,128)(2,1)} %bitcast.3), custom_call_target="tpu_custom_call" | custom-call | bytes 1600000 | tf_op jit(solution)/shard_map/pick_source/pallas_call | solution.py:40
  1.9 4.5 %collective-permute-start.7 = (bf16[2,6,2,128,128]{4,3,2,1,0:T(8,128)(2,1)S(1)}, bf16[2,6,2,128,128]{4,3,2,1,0:T(8,128)(2,1)S(1)}, u32[]{:S(2)}, u32[]{:S(2)}) collective-permute-start(bf16[2,6,2,128,128]{4,3,2,1,0:T(8,128)(2,1)S(1)} %pick_source.1.refs_9_.refs_10_), channel_id=1, source_target_pairs={{8,0},{10,2},{4,12},{6,14},{9,1},{11,3},{5,13},{7,15},{24,16},{26,... | collective-permute-start | bytes 2359304 | tf_op jit(solution)/shard_map/ppermute | solution.py:401
  6.5 0.1 collective-permute-start.6
  6.6 0.0 copy-done.2
  6.6 0.1 copy.7
  6.7 0.1 reshape.10.refs_5_.refs_7_
  6.8 0.6 collective-permute-start.11
  7.3 1.3 %collective-permute-start.9 = (s32[48]{0:T(128)S(1)}, s32[48]{0:T(128)S(1)}, u32[]{:S(2)}, u32[]{:S(2)}) collective-permute-start(s32[48]{0:T(128)S(1)} %reshape.10.refs_5_.refs_7_), channel_id=1, source_target_pairs={{8,0},{10,2},{4,12},{6,14},{9,1},{11,3},{5,13},{7,15},{24,16},{26,... | collective-permute-start | bytes 584 | tf_op jit(solution)/shard_map/ppermute | solution.py:401
  8.6 0.1 collective-permute-start.13
  8.7 0.0 collective-permute-done.6.other_ref.refs_2_.refs_3_
  8.7 1.9 %plan.1 = (s32[4]{0:T(128)}, s32[8]{0:T(128)}, s32[1]{0:T(128)}, f32[4,8,128]{2,1,0:T(8,128)S(1)}) custom-call(s32[1]{0:T(128)} %bitcast.core_ref, s32[1]{0:T(128)S(6)} %copy.25.own_ref.source_ref.refs_2_.refs_3_, s32[1]{0:T(128)} %collective-permute-done.6.other_ref.refs_2_.refs_3_, s32[4]{0:T(128)} %deltas_ref.1), custom_call_target="tpu_custom_call" | custom-call | bytes 1000 | tf_op jit(solution)/shard_map/plan/pallas_call | solution.py:130
  10.6 0.0 copy-start
  10.7 0.6 copy-done
  11.3 0.0 copy-start.1
  11.3 2.2 %pick_others.1 = (bf16[2,6,2,128,128]{4,3,2,1,0:T(8,128)(2,1)S(1)}, bf16[2,6,2,128,128]{4,3,2,1,0:T(8,128)(2,1)S(1)}, bf16[2,3,2,128,128]{4,3,2,1,0:T(8,128)(2,1)S(1)}, bf16[2,3,2,128,128]{4,3,2,1,0:T(8,128)(2,1)S(1)}) custom-call(s32[4]{0:T(128)S(1)} %copy-done, bf16[4,2,6,2,128,128]{5,4,3,2,1,0:T(8,128)(2,1)} %bitcast.4), custom_call_target="tpu_custom_call" | custom-call | bytes 5000000 | tf_op jit(solution)/shard_map/pick_others/pallas_call | solution.py:68
  13.5 1.3 %collective-permute-start.14 = (bf16[2,6,2,128,128]{4,3,2,1,0:T(8,128)(2,1)S(1)}, bf16[2,6,2,128,128]{4,3,2,1,0:T(8,128)(2,1)S(1)}, u32[]{:S(2)}, u32[]{:S(2)}) collective-permute-start(bf16[2,6,2,128,128]{4,3,2,1,0:T(8,128)(2,1)S(1)} %get-tuple-element.108.refs_11_), channel_id=1, source_target_pairs={{8,0},{10,2},{4,12},{6,14},{9,1},{11,3},{5,13},{7,15},{24,16},{26,... | collective-permute-start | bytes 2359304 | tf_op jit(solution)/shard_map/ppermute | solution.py:401
  15.4 9.0 %collective-permute-done.9.refs_4_.refs_6_ = s32[48]{0:T(128)S(1)} collective-permute-done((s32[48]{0:T(128)S(1)}, s32[48]{0:T(128)S(1)}, u32[]{:S(2)}, u32[]{:S(2)}) %collective-permute-start.9) | collective-permute-done | bytes 224 | tf_op jit(solution)/shard_map/ppermute | solution.py:401
  24.4 0.0 collective-permute-start.10
  24.4 0.0 collective-permute-done.7.refs_8_.refs_0_
  24.4 6.2 %collective-permute-start.8 = (bf16[2,6,2,128,128]{4,3,2,1,0:T(8,128)(2,1)S(1)}, bf16[2,6,2,128,128]{4,3,2,1,0:T(8,128)(2,1)}, u32[]{:S(2)}, u32[]{:S(2)}) collective-permute-start(bf16[2,6,2,128,128]{4,3,2,1,0:T(8,128)(2,1)S(1)} %get-tuple-element.104.refs_12_), channel_id=1, source_target_pairs={{8,0},{10,2},{4,12},{6,14},{9,1},{11,3},{5,13},{7,15},{24,16},{26,... | collective-permute-start | bytes 2359304 | tf_op jit(solution)/shard_map/ppermute | solution.py:401
  30.6 0.0 collective-permute-done.11.refs_5_
  30.6 0.2 collective-permute-start.12
  30.8 0.0 copy-done.1
  30.8 8.0 %weights.2.refs_1_ = f32[4,6,2,2,128,128]{5,4,3,2,1,0:T(8,128)S(1)} custom-call(s32[4]{0:T(128)S(1)} %copy-done, s32[8]{0:T(128)S(1)} %copy-done.1, s32[1]{0:T(128)S(6)} %copy.25.own_ref.source_ref.refs_2_.refs_3_, s32[1]{0:T(128)S(6)} %copy.25.own_ref.source_ref.refs_2_.refs_3_, s32[48]{0:T(128)S(1)} %collective-permute-done.9.refs_4_.refs_6_, ...), custom_call_target="tpu_custom_call" | custom-call | flops 80000000000 | bytes 4000000 | tf_op jit(solution)/shard_map/weights/pallas_call | solution.py:262
  38.8 0.0 collective-permute-done.10.refs_4_
  38.8 0.0 collective-permute-done.13.refs_9_
  38.8 0.0 collective-permute-done.12.refs_8_
  38.8 9.2 %weights.3.refs_2_ = f32[4,6,2,2,128,128]{5,4,3,2,1,0:T(8,128)S(1)} custom-call(s32[4]{0:T(128)S(1)} %copy-done, s32[8]{0:T(128)S(1)} %copy-done.1, s32[1]{0:T(128)} %collective-permute-done.6.other_ref.refs_2_.refs_3_, s32[1]{0:T(128)} %collective-permute-done.6.other_ref.refs_2_.refs_3_, s32[48]{0:T(128)S(1)} %collective-permute-done.10.refs_4_, ...), custom_call_target="tpu_custom_call" | custom-call | flops 2000000000 | bytes 4000000 | tf_op jit(solution)/shard_map/weights/pallas_call | solution.py:262
  48.1 0.5 inner.14.refs_4_
  48.6 0.0 collective-permute-done.14.refs_0_
  48.6 0.5 inner.15
  49.2 24.9 %conditional.1 = (f32[8,8,128]{2,1,0:T(8,128)S(1)}, f32[1,6,2,2,128,128]{5,4,3,2,1,0:T(8,128)S(1)}, f32[1,6,2,2,128,128]{5,4,3,2,1,0:T(8,128)S(1)}, f32[1,8,128]{2,1,0:T(8,128)S(1)}) conditional(s32[]{:T(128)} %bitcast.2, (f32[4,6,2,2,128,128]{5,4,3,2,1,0:T(8,128)S(1)}, f32[4,6,2,2,128,128]{5,4,3,2,1,0:T(8,128)S(1)}, ...), branch_computations={%region_0.0_spmd, %region_1.0_spmd, %region_2.0_spmd, %region_3.0_... | conditional | flops 8000000 | bytes 17145840 | solution.py:477
  49.2 1.3 %collective-permute-start.5 = (bf16[2,3,2,128,128]{4,3,2,1,0:T(8,128)(2,1)S(1)}, bf16[2,3,2,128,128]{4,3,2,1,0:T(8,128)(2,1)S(1)}, u32[]{:S(2)}, u32[]{:S(2)}) collective-permute-start(bf16[2,3,2,128,128]{4,3,2,1,0:T(8,128)(2,1)S(1)} %get-tuple-element.78), channel_id=1, source_target_pairs={{8,0},{9,1},{10,2},{11,3},{4,12},{5,13},{6,14},{7,15},{24,16},{25,... | collective-permute-start | bytes 1179656 | tf_op jit(solution)/shard_map/cond/branch_3_fun/ppermute | solution.py:466
  50.5 1.3 %collective-permute-start.4 = (bf16[2,3,2,128,128]{4,3,2,1,0:T(8,128)(2,1)S(1)}, bf16[2,3,2,128,128]{4,3,2,1,0:T(8,128)(2,1)S(1)}, u32[]{:S(2)}, u32[]{:S(2)}) collective-permute-start(bf16[2,3,2,128,128]{4,3,2,1,0:T(8,128)(2,1)S(1)} %get-tuple-element.74), channel_id=1, source_target_pairs={{8,0},{9,1},{10,2},{11,3},{4,12},{5,13},{6,14},{7,15},{24,16},{25,... | collective-permute-start | bytes 1179656 | tf_op jit(solution)/shard_map/cond/branch_3_fun/ppermute | solution.py:466
  51.8 0.4 stage.7
  52.2 14.3 %collective-permute-done.5.refs_0_ = bf16[2,3,2,128,128]{4,3,2,1,0:T(8,128)(2,1)S(1)} collective-permute-done((bf16[2,3,2,128,128]{4,3,2,1,0:T(8,128)(2,1)S(1)}, bf16[2,3,2,128,128]{4,3,2,1,0:T(8,128)(2,1)S(1)}, u32[]{:S(2)}, u32[]{:S(2)}) %collective-permute-start.5) | collective-permute-done | bytes 393248 | tf_op jit(solution)/shard_map/cond/branch_3_fun/ppermute | solution.py:466
  66.5 0.3 inner.12.refs_4_
  66.8 7.0 %collective-permute-done.4.refs_0_ = bf16[2,3,2,128,128]{4,3,2,1,0:T(8,128)(2,1)S(1)} collective-permute-done((bf16[2,3,2,128,128]{4,3,2,1,0:T(8,128)(2,1)S(1)}, bf16[2,3,2,128,128]{4,3,2,1,0:T(8,128)(2,1)S(1)}, u32[]{:S(2)}, u32[]{:S(2)}) %collective-permute-start.4) | collective-permute-done | bytes 393248 | tf_op jit(solution)/shard_map/cond/branch_3_fun/ppermute | solution.py:466
  73.8 0.3 inner.13
  74.1 0.0 collective-permute-done.8.field_ref
  74.1 1.7 %last.1 = (f32[2,2,1]{2,1,0:T(2,128)S(1)}, f32[2,2,1]{2,1,0:T(2,128)S(1)}) custom-call(bf16[2,6,2,128,128]{4,3,2,1,0:T(8,128)(2,1)} %collective-permute-done.8.field_ref, f32[1,6,2,2,128,128]{5,4,3,2,1,0:T(8,128)S(1)} %get-tuple-element.115.u0_ref, f32[1,6,2,2,128,128]{5,4,3,2,1,0:T(8,128)S(1)} %get-tuple-element.116.u1_ref, ...), custom_call_target="tpu_custom_call" | custom-call | flops 4000000 | bytes 4000000 | tf_op jit(solution)/shard_map/last/pallas_call | solution.py:382
  75.8 0.0 collective-permute-start.15
  75.8 1.1 %collective-permute-done.15 = f32[2,2,1]{2,1,0:T(2,128)S(1)} collective-permute-done((f32[2,2,1]{2,1,0:T(2,128)S(1)}, f32[2,2,1]{2,1,0:T(2,128)S(1)}, u32[]{:S(2)}, u32[]{:S(2)}) %collective-permute-start.15) | collective-permute-done | bytes 48 | tf_op jit(solution)/shard_map/ppermute | solution.py:400
  76.9 1.3 %collective-permute-start.16 = (f32[2,2,1]{2,1,0:T(2,128)S(1)}, f32[2,2,1]{2,1,0:T(2,128)S(1)}, u32[]{:S(2)}, u32[]{:S(2)}) collective-permute-start(f32[2,2,1]{2,1,0:T(2,128)S(1)} %add.6), channel_id=1, source_target_pairs={{0,8},{1,9},{2,10},{3,11},{12,4},{13,5},{14,6},{15,7},{16,24},{17,... | collective-permute-start | bytes 56 | tf_op jit(solution)/shard_map/ppermute | solution.py:482
  78.2 5.1 %collective-permute-done.16 = f32[2,2,1]{2,1,0:T(2,128)S(1)} collective-permute-done((f32[2,2,1]{2,1,0:T(2,128)S(1)}, f32[2,2,1]{2,1,0:T(2,128)S(1)}, u32[]{:S(2)}, u32[]{:S(2)}) %collective-permute-start.16) | collective-permute-done | bytes 48 | tf_op jit(solution)/shard_map/ppermute | solution.py:482
  83.3 0.7 copy.8
  (2 shorter events, 0.0 us)
Async XLA Ops:
  0.7 5.9 %copy-start.2 = (s32[1,4,6,2]{2,3,1,0:T(2,128)S(1)}, s32[1,4,6,2]{2,3,1,0:T(2,128)}, u32[]{:S(2)}) copy-start(s32[1,4,6,2]{2,3,1,0:T(2,128)} %param.10) | copy-start | bytes 580
  1.9 22.5 %collective-permute-start.7 = (bf16[2,6,2,128,128]{4,3,2,1,0:T(8,128)(2,1)S(1)}, bf16[2,6,2,128,128]{4,3,2,1,0:T(8,128)(2,1)S(1)}, u32[]{:S(2)}, u32[]{:S(2)}) collective-permute-start(bf16[2,6,2,128,128]{4,3,2,1,0:T(8,128)(2,1)S(1)} %pick_source.1.refs_9_.refs_10_), channel_id=1, source_target_pairs={{8,0},{10,2},{4,12},{6,14},{9,1},{11,3},{5,13},{7,15},{24,16},{26,... | collective-permute-start | bytes 2359304 | tf_op jit(solution)/shard_map/ppermute | solution.py:401
  6.5 2.2 %collective-permute-start.6 = (s32[1]{0:T(128)}, s32[1]{0:T(128)}, u32[]{:S(2)}, u32[]{:S(2)}) collective-permute-start(s32[1]{0:T(128)} %param.11), channel_id=1, source_target_pairs={{0,1},{1,0},{2,3},{3,2},{4,5},{5,4},{6,7},{7,6},{8,9},{9,8},{10,11... | collective-permute-start | bytes 20 | tf_op jit(solution)/shard_map/ppermute | solution.py:400
  6.8 23.8 %collective-permute-start.11 = (s32[48]{0:T(128)S(1)}, s32[48]{0:T(128)S(1)}, u32[]{:S(2)}, u32[]{:S(2)}) collective-permute-start(s32[48]{0:T(128)S(1)} %reshape.10.refs_5_.refs_7_), channel_id=1, source_target_pairs={{0,1},{1,0},{2,3},{3,2},{4,5},{5,4},{6,7},{7,6},{8,9},{9,8},{10,11... | collective-permute-start | bytes 584 | tf_op jit(solution)/shard_map/ppermute | solution.py:400
  7.3 17.1 %collective-permute-start.9 = (s32[48]{0:T(128)S(1)}, s32[48]{0:T(128)S(1)}, u32[]{:S(2)}, u32[]{:S(2)}) collective-permute-start(s32[48]{0:T(128)S(1)} %reshape.10.refs_5_.refs_7_), channel_id=1, source_target_pairs={{8,0},{10,2},{4,12},{6,14},{9,1},{11,3},{5,13},{7,15},{24,16},{26,... | collective-permute-start | bytes 584 | tf_op jit(solution)/shard_map/ppermute | solution.py:401
  8.6 30.2 %collective-permute-start.13 = (bf16[2,6,2,128,128]{4,3,2,1,0:T(8,128)(2,1)S(1)}, bf16[2,6,2,128,128]{4,3,2,1,0:T(8,128)(2,1)S(1)}, u32[]{:S(2)}, u32[]{:S(2)}) collective-permute-start(bf16[2,6,2,128,128]{4,3,2,1,0:T(8,128)(2,1)S(1)} %pick_source.1.refs_9_.refs_10_), channel_id=1, source_target_pairs={{0,1},{1,0},{2,3},{3,2},{4,5},{5,4},{6,7},{7,6},{8,9},{9,8},{10,11... | collective-permute-start | bytes 2359304 | tf_op jit(solution)/shard_map/ppermute | solution.py:400
  10.6 0.6 copy-start
  11.3 19.6 %copy-start.1 = (s32[8]{0:T(128)S(1)}, s32[8]{0:T(128)}, u32[]{:S(2)}) copy-start(s32[8]{0:T(128)} %get-tuple-element.106.refs_1_) | copy-start | bytes 100
  13.5 35.2 %collective-permute-start.14 = (bf16[2,6,2,128,128]{4,3,2,1,0:T(8,128)(2,1)S(1)}, bf16[2,6,2,128,128]{4,3,2,1,0:T(8,128)(2,1)S(1)}, u32[]{:S(2)}, u32[]{:S(2)}) collective-permute-start(bf16[2,6,2,128,128]{4,3,2,1,0:T(8,128)(2,1)S(1)} %get-tuple-element.108.refs_11_), channel_id=1, source_target_pairs={{8,0},{10,2},{4,12},{6,14},{9,1},{11,3},{5,13},{7,15},{24,16},{26,... | collective-permute-start | bytes 2359304 | tf_op jit(solution)/shard_map/ppermute | solution.py:401
  24.4 14.4 %collective-permute-start.10 = (s32[48]{0:T(128)S(1)}, s32[48]{0:T(128)S(1)}, u32[]{:S(2)}, u32[]{:S(2)}) collective-permute-start(s32[48]{0:T(128)S(1)} %collective-permute-done.9.refs_4_.refs_6_), channel_id=1, source_target_pairs={{0,1},{1,0},{2,3},{3,2},{4,5},{5,4},{6,7},{7,6},{8,9},{9,8},{10,11... | collective-permute-start | bytes 584 | tf_op jit(solution)/shard_map/ppermute | solution.py:400
  24.4 49.6 %collective-permute-start.8 = (bf16[2,6,2,128,128]{4,3,2,1,0:T(8,128)(2,1)S(1)}, bf16[2,6,2,128,128]{4,3,2,1,0:T(8,128)(2,1)}, u32[]{:S(2)}, u32[]{:S(2)}) collective-permute-start(bf16[2,6,2,128,128]{4,3,2,1,0:T(8,128)(2,1)S(1)} %get-tuple-element.104.refs_12_), channel_id=1, source_target_pairs={{8,0},{10,2},{4,12},{6,14},{9,1},{11,3},{5,13},{7,15},{24,16},{26,... | collective-permute-start | bytes 2359304 | tf_op jit(solution)/shard_map/ppermute | solution.py:401
  30.6 8.2 %collective-permute-start.12 = (bf16[2,6,2,128,128]{4,3,2,1,0:T(8,128)(2,1)S(1)}, bf16[2,6,2,128,128]{4,3,2,1,0:T(8,128)(2,1)S(1)}, u32[]{:S(2)}, u32[]{:S(2)}) collective-permute-start(bf16[2,6,2,128,128]{4,3,2,1,0:T(8,128)(2,1)S(1)} %collective-permute-done.7.refs_8_.refs_0_), channel_id=1, source_target_pairs={{0,1},{1,0},{2,3},{3,2},{4,5},{5,4},{6,7},{7,6},{8,9},{9,8},{10,11... | collective-permute-start | bytes 2359304 | tf_op jit(solution)/shard_map/ppermute | solution.py:400
  49.2 17.3 %collective-permute-start.5 = (bf16[2,3,2,128,128]{4,3,2,1,0:T(8,128)(2,1)S(1)}, bf16[2,3,2,128,128]{4,3,2,1,0:T(8,128)(2,1)S(1)}, u32[]{:S(2)}, u32[]{:S(2)}) collective-permute-start(bf16[2,3,2,128,128]{4,3,2,1,0:T(8,128)(2,1)S(1)} %get-tuple-element.78), channel_id=1, source_target_pairs={{8,0},{9,1},{10,2},{11,3},{4,12},{5,13},{6,14},{7,15},{24,16},{25,... | collective-permute-start | bytes 1179656 | tf_op jit(solution)/shard_map/cond/branch_3_fun/ppermute | solution.py:466
  50.5 23.3 %collective-permute-start.4 = (bf16[2,3,2,128,128]{4,3,2,1,0:T(8,128)(2,1)S(1)}, bf16[2,3,2,128,128]{4,3,2,1,0:T(8,128)(2,1)S(1)}, u32[]{:S(2)}, u32[]{:S(2)}) collective-permute-start(bf16[2,3,2,128,128]{4,3,2,1,0:T(8,128)(2,1)S(1)} %get-tuple-element.74), channel_id=1, source_target_pairs={{8,0},{9,1},{10,2},{11,3},{4,12},{5,13},{6,14},{7,15},{24,16},{25,... | collective-permute-start | bytes 1179656 | tf_op jit(solution)/shard_map/cond/branch_3_fun/ppermute | solution.py:466
  75.8 1.2 %collective-permute-start.15 = (f32[2,2,1]{2,1,0:T(2,128)S(1)}, f32[2,2,1]{2,1,0:T(2,128)S(1)}, u32[]{:S(2)}, u32[]{:S(2)}) collective-permute-start(f32[2,2,1]{2,1,0:T(2,128)S(1)} %get-tuple-element.120), channel_id=1, source_target_pairs={{0,1},{1,0},{2,3},{3,2},{4,5},{5,4},{6,7},{7,6},{8,9},{9,8},{10,11... | collective-permute-start | bytes 56 | tf_op jit(solution)/shard_map/ppermute | solution.py:400
  76.9 6.4 %collective-permute-start.16 = (f32[2,2,1]{2,1,0:T(2,128)S(1)}, f32[2,2,1]{2,1,0:T(2,128)S(1)}, u32[]{:S(2)}, u32[]{:S(2)}) collective-permute-start(f32[2,2,1]{2,1,0:T(2,128)S(1)} %add.6), channel_id=1, source_target_pairs={{0,8},{1,9},{2,10},{3,11},{12,4},{13,5},{14,6},{15,7},{16,24},{17,... | collective-permute-start | bytes 56 | tf_op jit(solution)/shard_map/ppermute | solution.py:482

commit v2 on v1

--- a/solution.py
+++ b/solution.py
@@ -366,8 +366,8 @@
     )(u0, u1, masks)
 
 
-def last_kernel(field_ref, u0_ref, u1_ref, masks_ref, before_ref, mine_ref, theirs_ref):
-    lines = add_lines(0, 0, field_ref, u0_ref, u1_ref, masks_ref, before_ref)
+def last_kernel(first, field_ref, u0_ref, u1_ref, masks_ref, before_ref, mine_ref, theirs_ref):
+    lines = add_lines(0, first, field_ref, u0_ref, u1_ref, masks_ref, before_ref)
     table = jnp.concatenate([jnp.sum(line, axis=0, keepdims=True) for line in lines], axis=0)
     table = jnp.sum(table, axis=1, keepdims=True)
     share = mine_ref.shape[1]
@@ -377,10 +377,10 @@
         theirs_ref[part] = table[at + share : at + 2 * share]
 
 
-def last(field, u0, u1, masks, lines):
+def last(first, field, u0, u1, masks, lines):
     share = masks.shape[1] // 4
     return pl.pallas_call(
-        last_kernel,
+        lambda *refs: last_kernel(first, *refs),
         out_shape=[jax.ShapeDtypeStruct((2, share, 1), F32)] * 2,
         in_specs=[VMEM] * 5,
         out_specs=[VMEM] * 2,
@@ -409,18 +409,19 @@
     order, active, full, masks = plan(core, sources, other_time, deltas, times)
     rows = fields.shape[2]
     half = rows // 2
-    pieces = [(slot, 0, rows) for slot in range(times - 1)]
-    pieces += [(times - 1, 0, half), (times - 1, half, rows - half)]
+    halves = [(0, half), (half, rows - half)]
+    pieces = [(slot, 0, rows) for slot in range(times - 2)]
+    pieces += [(slot, *part) for slot in (times - 2, times - 1) for part in halves]
     picked = [own_field, *pick_others(order, fields, pieces[1:])]
-    *early, near, late_low, late_high = picked
+    *early, near_low, near_high, late_low, late_high = picked
     far += [to_partner(field) for field in early[1:]]
-    near, far[0] = lax.optimization_barrier((near, far[0]))
-    near = to_partner(near)
-
     other_cols = swap(cols)
     far_other_cols = swap(far_cols)
     other_field = swap(own_field)
     far_other = swap(far[0])
+    near_low, far[0] = lax.optimization_barrier((near_low, far[0]))
+    near_high, far_other = lax.optimization_barrier((near_high, far_other))
+    near_low, near_high = to_partner(near_low), to_partner(near_high)
     u0 = weights(
         80_000_000_000,
         0,
@@ -475,7 +476,8 @@
     branches = [without_slot, with_slot([0]), with_slot([1]), with_slot([0, 1])]
     late_low, late_high, lines = lax.optimization_barrier((late_low, late_high, lines))
     lines, *staged = lax.switch(full[0], branches, late_low, late_high, u0, u1, masks, lines)
-    mine, theirs = last(near, *staged, lines)
+    lines = inner(0, 0, near_low, *staged, lines)
+    mine, theirs = last(half, near_high, *staged, lines)
 
     total = mine + swap(theirs)
     back = [(2 * a + c, 2 * b + c) for b, a in pairs for c in range(2)]

time: 84.4 us -> 91.4 us (1.083)
  Pallas kernels: 26.2 us -> 32.1 us
  starting transfers between devices: 18.2 us -> 20.4 us
  waiting for transfers between devices: 36.5 us -> 35.4 us
    ppermute x4 -> x5, waiting for transfers between devices: 9 us -> 16.7 us  [local(): to_partner = lambda value: lax.ppermute(value, 'mom', pairs)]
    ppermute x1, waiting for transfers between devices: 14.3 us -> 9.22 us  [branch(): lax.ppermute(low, both, routes)]
    ppermute x1, waiting for transfers between devices: 7.01 us -> 3.19 us  [branch(): lax.ppermute(high, both, routes)]
    pallas_call x4 -> x5, Pallas kernels: 1.58 us -> 4.81 us  [inner(): pl.pallas_call(lambda *refs: inner_kernel(slot, first, *refs), out_shape=...]
    pallas_call x2, Pallas kernels: 17.2 us -> 19.4 us  [weights(): pl.pallas_call(lambda *refs: weights_kernel(s, pieces, *refs), out_shape=...]
    ppermute x4 -> x5, starting transfers between devices: 13.4 us -> 15.6 us  [local(): to_partner = lambda value: lax.ppermute(value, 'mom', pairs)]
  transfers between devices with their start and end apart: 13 -> 14, of which waited for: 5 -> 5; matrix products, arithmetic and copies ran while one was open for 0% -> 0% of each run, Pallas kernels for 28% -> 33%
where the time goes in v2:
time: 91.4 us; the launch traced here: 90.9 us
  waiting for transfers between devices  35.4 us (39%)
  Pallas kernels  32.1 us (35%)
  starting transfers between devices  20.4 us (22%)
  local copies, waits for them, and re-layouts  1.54 us (2%)
  between operations  1.45 us (2%)
    pallas_call x2, Pallas kernels, weights(): pl.pallas_call(lambda *refs: weights_kernel(s, pieces, *refs), out_shape=...  19.4 us
    ppermute x5, waiting for transfers between devices, local(): to_partner = lambda value: lax.ppermute(value, 'mom', pairs)  16.7 us
    ppermute x5, starting transfers between devices, local(): to_partner = lambda value: lax.ppermute(value, 'mom', pairs)  15.6 us
    ppermute x1, waiting for transfers between devices, branch(): lax.ppermute(low, both, routes)  9.22 us
    ppermute x1, waiting for transfers between devices, local(): return total + lax.ppermute(total, both, back)  5.08 us
    pallas_call x5, Pallas kernels, inner(): pl.pallas_call(lambda *refs: inner_kernel(slot, first, *refs), out_shape=...  4.81 us
    ppermute x1, waiting for transfers between devices, branch(): lax.ppermute(high, both, routes)  3.19 us
    pallas_call x1, Pallas kernels, pick_others(): pl.pallas_call(lambda *refs: pick_kernel(pieces, *refs), out_shape=[jax.S...  2.95 us
  transfers between devices with their start and end apart: 14, of which 5 were waited for; matrix products, arithmetic and copies ran while one was open for 0% of the time, Pallas kernels for 33%

profile of v2, /device:TPU:8, one launch (start us, length us, event | category | flops | bytes accessed | tf_op | source)
XLA Modules:
  0.0 90.9 jit_solution(15714860919719589731)
XLA Ops:
  0.7 0.0 copy-start.3
  0.7 1.3 %pick_source.1.refs_9_.refs_10_ = bf16[2,6,2,128,128]{4,3,2,1,0:T(8,128)(2,1)S(1)} custom-call(s32[1]{0:T(128)S(6)} %copy.25.own_ref.source_ref.refs_2_.refs_3_, bf16[4,2,6,2,128,128]{5,4,3,2,1,0:T(8,128)(2,1)} %bitcast.3), custom_call_target="tpu_custom_call" | custom-call | bytes 1600000 | tf_op jit(solution)/shard_map/pick_source/pallas_call | solution.py:40
  1.9 4.5 %collective-permute-start.7 = (bf16[2,6,2,128,128]{4,3,2,1,0:T(8,128)(2,1)S(1)}, bf16[2,6,2,128,128]{4,3,2,1,0:T(8,128)(2,1)S(1)}, u32[]{:S(2)}, u32[]{:S(2)}) collective-permute-start(bf16[2,6,2,128,128]{4,3,2,1,0:T(8,128)(2,1)S(1)} %pick_source.1.refs_9_.refs_10_), channel_id=1, source_target_pairs={{8,0},{10,2},{4,12},{6,14},{9,1},{11,3},{5,13},{7,15},{24,16},{26,... | collective-permute-start | bytes 2359304 | tf_op jit(solution)/shard_map/ppermute | solution.py:401
  6.5 16.7 %collective-permute-done.7.refs_8_.refs_0_ = bf16[2,6,2,128,128]{4,3,2,1,0:T(8,128)(2,1)S(1)} collective-permute-done((bf16[2,6,2,128,128]{4,3,2,1,0:T(8,128)(2,1)S(1)}, bf16[2,6,2,128,128]{4,3,2,1,0:T(8,128)(2,1)S(1)}, u32[]{:S(2)}, u32[]{:S(2)}) %collective-permute-start.7) | collective-permute-done | bytes 786464 | tf_op jit(solution)/shard_map/ppermute | solution.py:401
  23.2 0.0 collective-permute-start.8
  23.2 0.5 collective-permute-start.6
  23.7 0.0 copy-done.3
  23.7 0.1 copy.7
  23.8 0.1 reshape.10.refs_5_.refs_7_
  23.9 0.1 collective-permute-start.12
  24.0 5.3 %collective-permute-start.10 = (s32[48]{0:T(128)S(1)}, s32[48]{0:T(128)S(1)}, u32[]{:S(2)}, u32[]{:S(2)}) collective-permute-start(s32[48]{0:T(128)S(1)} %reshape.10.refs_5_.refs_7_), channel_id=1, source_target_pairs={{8,0},{10,2},{4,12},{6,14},{9,1},{11,3},{5,13},{7,15},{24,16},{26,... | collective-permute-start | bytes 584 | tf_op jit(solution)/shard_map/ppermute | solution.py:401
  29.3 0.3 collective-permute-start.13
  29.6 0.0 collective-permute-done.6.other_ref.refs_2_.refs_3_
  29.6 2.0 %plan.1 = (s32[4]{0:T(128)}, s32[8]{0:T(128)}, s32[1]{0:T(128)}, f32[4,8,128]{2,1,0:T(8,128)}) custom-call(s32[1]{0:T(128)} %bitcast.core_ref, s32[1]{0:T(128)S(6)} %copy.25.own_ref.source_ref.refs_2_.refs_3_, s32[1]{0:T(128)} %collective-permute-done.6.other_ref.refs_2_.refs_3_, s32[4]{0:T(128)} %deltas_ref.1), custom_call_target="tpu_custom_call" | custom-call | bytes 1000 | tf_op jit(solution)/shard_map/plan/pallas_call | solution.py:130
  31.6 0.7 copy-done
  32.2 2.9 %pick_others.1 = (bf16[2,6,2,128,128]{4,3,2,1,0:T(8,128)(2,1)S(1)}, bf16[2,3,2,128,128]{4,3,2,1,0:T(8,128)(2,1)}, bf16[2,3,2,128,128]{4,3,2,1,0:T(8,128)(2,1)S(1...) custom-call(s32[4]{0:T(128)S(1)} %copy-done, bf16[4,2,6,2,128,128]{5,4,3,2,1,0:T(8,128)(2,1)} %bitcast.4), custom_call_target="tpu_custom_call" | custom-call | bytes 5000000 | tf_op jit(solution)/shard_map/pick_others/pallas_call | solution.py:68
  35.2 1.6 %collective-permute-start.14 = (bf16[2,6,2,128,128]{4,3,2,1,0:T(8,128)(2,1)S(1)}, bf16[2,6,2,128,128]{4,3,2,1,0:T(8,128)(2,1)S(1)}, u32[]{:S(2)}, u32[]{:S(2)}) collective-permute-start(bf16[2,6,2,128,128]{4,3,2,1,0:T(8,128)(2,1)S(1)} %get-tuple-element.112.refs_11_), channel_id=1, source_target_pairs={{8,0},{10,2},{4,12},{6,14},{9,1},{11,3},{5,13},{7,15},{24,16},{26,... | collective-permute-start | bytes 2359304 | tf_op jit(solution)/shard_map/ppermute | solution.py:401
  37.4 0.0 collective-permute-done.10.refs_4_.refs_6_
  37.5 0.1 collective-permute-start.11
  37.5 0.0 collective-permute-done.8.refs_8_
  37.5 2.1 %collective-permute-start.15 = (bf16[2,3,2,128,128]{4,3,2,1,0:T(8,128)(2,1)}, bf16[2,3,2,128,128]{4,3,2,1,0:T(8,128)(2,1)}, u32[]{:S(2)}, u32[]{:S(2)}) collective-permute-start(bf16[2,3,2,128,128]{4,3,2,1,0:T(8,128)(2,1)} %get-tuple-element.123.refs_12_), channel_id=1, source_target_pairs={{8,0},{10,2},{4,12},{6,14},{9,1},{11,3},{5,13},{7,15},{24,16},{26,... | collective-permute-start | bytes 1179656 | tf_op jit(solution)/shard_map/ppermute | solution.py:401
  39.6 0.0 collective-permute-done.12.refs_5_
  39.6 2.1 %collective-permute-start.9 = (bf16[2,3,2,128,128]{4,3,2,1,0:T(8,128)(2,1)S(1)}, bf16[2,3,2,128,128]{4,3,2,1,0:T(8,128)(2,1)}, u32[]{:S(2)}, u32[]{:S(2)}) collective-permute-start(bf16[2,3,2,128,128]{4,3,2,1,0:T(8,128)(2,1)S(1)} %get-tuple-element.107.refs_13_), channel_id=1, source_target_pairs={{8,0},{10,2},{4,12},{6,14},{9,1},{11,3},{5,13},{7,15},{24,16},{26,... | collective-permute-start | bytes 1179656 | tf_op jit(solution)/shard_map/ppermute | solution.py:401
  41.7 0.0 copy-done.1
  41.7 8.1 %weights.2.refs_1_ = f32[4,6,2,2,128,128]{5,4,3,2,1,0:T(8,128)S(1)} custom-call(s32[4]{0:T(128)S(1)} %copy-done, s32[8]{0:T(128)S(1)} %copy-done.1, s32[1]{0:T(128)S(6)} %copy.25.own_ref.source_ref.refs_2_.refs_3_, s32[1]{0:T(128)S(6)} %copy.25.own_ref.source_ref.refs_2_.refs_3_, s32[48]{0:T(128)S(1)} %collective-permute-done.10.refs_4_.refs_6_, ...), custom_call_target="tpu_custom_call" | custom-call | flops 80000000000 | bytes 4000000 | tf_op jit(solution)/shard_map/weights/pallas_call | solution.py:262
  49.8 0.0 collective-permute-done.11.refs_4_
  49.8 0.0 collective-permute-done.13.refs_9_
  49.8 11.3 %weights.3.refs_2_ = f32[4,6,2,2,128,128]{5,4,3,2,1,0:T(8,128)S(1)} custom-call(s32[4]{0:T(128)S(1)} %copy-done, s32[8]{0:T(128)S(1)} %copy-done.1, s32[1]{0:T(128)} %collective-permute-done.6.other_ref.refs_2_.refs_3_, s32[1]{0:T(128)} %collective-permute-done.6.other_ref.refs_2_.refs_3_, s32[48]{0:T(128)S(1)} %collective-permute-done.11.refs_4_, ...), custom_call_target="tpu_custom_call" | custom-call | flops 2000000000 | bytes 4000000 | tf_op jit(solution)/shard_map/weights/pallas_call | solution.py:262
  61.2 0.5 inner.15.refs_4_
  61.7 0.0 collective-permute-done.14.refs_0_
  61.7 1.1 %inner.16 = f32[8,8,128]{2,1,0:T(8,128)} custom-call(bf16[2,6,2,128,128]{4,3,2,1,0:T(8,128)(2,1)S(1)} %collective-permute-done.14.refs_0_, f32[4,6,2,2,128,128]{5,4,3,2,1,0:T(8,128)S(1)} %weights.2.refs_1_, f32[4,6,2,2,128,128]{5,4,3,2,1,0:T(8,128)S(1)} %weights.3.refs_2_, f32[4,8,128]{2,1,0:T(8,128)S(1)} %copy-done.2, f32[8,8,128]{2,1,0:T(8,128)S(1)} %inner.15.refs_4_), custom_call_target="tpu_custom_call" | custom-call | flops 4000000 | bytes 4000000 | tf_op jit(solution)/shard_map/inner/pallas_call | solution.py:331
  62.9 17.3 %conditional.1 = (f32[8,8,128]{2,1,0:T(8,128)}, f32[1,6,2,2,128,128]{5,4,3,2,1,0:T(8,128)S(1)}, f32[1,6,2,2,128,128]{5,4,3,2,1,0:T(8,128)S(1)}, f32[1,8,128]{2,1,0:T(8,128)S(1)}) conditional(s32[]{:T(128)} %bitcast.2, (f32[4,6,2,2,128,128]{5,4,3,2,1,0:T(8,128)S(1)}, f32[4,6,2,2,128,128]{5,4,3,2,1,0:T(8,128)S(1)}, ...), branch_computations={%region_0.0_spmd, %region_1.0_spmd, %region_2.0_spmd, %region_3.0_... | conditional | flops 8000000 | bytes 17145840 | solution.py:478
  62.9 1.3 %collective-permute-start.1 = (bf16[2,3,2,128,128]{4,3,2,1,0:T(8,128)(2,1)S(1)}, bf16[2,3,2,128,128]{4,3,2,1,0:T(8,128)(2,1)S(1)}, u32[]{:S(2)}, u32[]{:S(2)}) collective-permute-start(bf16[2,3,2,128,128]{4,3,2,1,0:T(8,128)(2,1)S(1)} %get-tuple-element.60), channel_id=1, source_target_pairs={{8,0},{10,2},{4,12},{6,14},{24,16},{26,18},{20,28},{22,30}} | collective-permute-start | bytes 1179656 | tf_op jit(solution)/shard_map/cond/branch_1_fun/ppermute | solution.py:467
  64.2 1.3 %collective-permute-start = (bf16[2,3,2,128,128]{4,3,2,1,0:T(8,128)(2,1)S(1)}, bf16[2,3,2,128,128]{4,3,2,1,0:T(8,128)(2,1)S(1)}, u32[]{:S(2)}, u32[]{:S(2)}) collective-permute-start(bf16[2,3,2,128,128]{4,3,2,1,0:T(8,128)(2,1)S(1)} %get-tuple-element.56), channel_id=1, source_target_pairs={{8,0},{10,2},{4,12},{6,14},{24,16},{26,18},{20,28},{22,30}} | collective-permute-start | bytes 1179656 | tf_op jit(solution)/shard_map/cond/branch_1_fun/ppermute | solution.py:467
  65.5 0.4 stage.5
  65.9 9.2 %collective-permute-done.1.refs_0_ = bf16[2,3,2,128,128]{4,3,2,1,0:T(8,128)(2,1)S(1)} collective-permute-done((bf16[2,3,2,128,128]{4,3,2,1,0:T(8,128)(2,1)S(1)}, bf16[2,3,2,128,128]{4,3,2,1,0:T(8,128)(2,1)S(1)}, u32[]{:S(2)}, u32[]{:S(2)}) %collective-permute-start.1) | collective-permute-done | bytes 393248 | tf_op jit(solution)/shard_map/cond/branch_1_fun/ppermute | solution.py:467
  75.1 1.0 %inner.9.refs_4_ = f32[8,8,128]{2,1,0:T(8,128)S(1)} custom-call(bf16[2,3,2,128,128]{4,3,2,1,0:T(8,128)(2,1)S(1)} %collective-permute-done.1.refs_0_, f32[4,6,2,2,128,128]{5,4,3,2,1,0:T(8,128)S(1)} %get-tuple-element.57.refs_1_.refs_0_, f32[4,6,2,2,128,128]{5,4,3,2,1,0:T(8,128)S(1)} %get-tuple-element.58.refs_2_.refs_1_, ...), custom_call_target="tpu_custom_call" | custom-call | flops 4000000 | bytes 4000000 | tf_op jit(solution)/shard_map/cond/branch_1_fun/inner/pallas_call | solution.py:331
  76.1 3.2 %collective-permute-done.refs_0_ = bf16[2,3,2,128,128]{4,3,2,1,0:T(8,128)(2,1)S(1)} collective-permute-done((bf16[2,3,2,128,128]{4,3,2,1,0:T(8,128)(2,1)S(1)}, bf16[2,3,2,128,128]{4,3,2,1,0:T(8,128)(2,1)S(1)}, u32[]{:S(2)}, u32[]{:S(2)}) %collective-permute-start) | collective-permute-done | bytes 393248 | tf_op jit(solution)/shard_map/cond/branch_1_fun/ppermute | solution.py:467
  79.3 0.9 inner.10
  80.2 0.0 collective-permute-done.15.refs_0_
  80.2 1.2 %inner.17.refs_4_ = f32[8,8,128]{2,1,0:T(8,128)S(1)} custom-call(bf16[2,3,2,128,128]{4,3,2,1,0:T(8,128)(2,1)} %collective-permute-done.15.refs_0_, f32[1,6,2,2,128,128]{5,4,3,2,1,0:T(8,128)S(1)} %get-tuple-element.120.refs_1_, f32[1,6,2,2,128,128]{5,4,3,2,1,0:T(8,128)S(1)} %get-tuple-element.121.refs_2_, f32[1,8,128]{2,1,0:T(8,128)S(1)} %get-tuple-element.122.refs_3_, ...), custom_call_target="tpu_custom_call" | custom-call | flops 4000000 | bytes 4000000 | tf_op jit(solution)/shard_map/inner/pallas_call | solution.py:331
  81.4 0.0 collective-permute-done.9.refs_0_
  81.4 1.3 %last.1 = (f32[2,2,1]{2,1,0:T(2,128)S(1)}, f32[2,2,1]{2,1,0:T(2,128)S(1)}) custom-call(bf16[2,3,2,128,128]{4,3,2,1,0:T(8,128)(2,1)} %collective-permute-done.9.refs_0_, f32[1,6,2,2,128,128]{5,4,3,2,1,0:T(8,128)S(1)} %get-tuple-element.120.refs_1_, f32[1,6,2,2,128,128]{5,4,3,2,1,0:T(8,128)S(1)} %get-tuple-element.121.refs_2_, ...), custom_call_target="tpu_custom_call" | custom-call | flops 4000000 | bytes 4000000 | tf_op jit(solution)/shard_map/last/pallas_call | solution.py:382
  82.8 0.0 collective-permute-start.16
  82.8 1.1 %collective-permute-done.16 = f32[2,2,1]{2,1,0:T(2,128)S(1)} collective-permute-done((f32[2,2,1]{2,1,0:T(2,128)S(1)}, f32[2,2,1]{2,1,0:T(2,128)S(1)}, u32[]{:S(2)}, u32[]{:S(2)}) %collective-permute-start.16) | collective-permute-done | bytes 48 | tf_op jit(solution)/shard_map/ppermute | solution.py:400
  83.9 1.3 %collective-permute-start.17 = (f32[2,2,1]{2,1,0:T(2,128)S(1)}, f32[2,2,1]{2,1,0:T(2,128)S(1)}, u32[]{:S(2)}, u32[]{:S(2)}) collective-permute-start(f32[2,2,1]{2,1,0:T(2,128)S(1)} %add.6), channel_id=1, source_target_pairs={{0,8},{1,9},{2,10},{3,11},{12,4},{13,5},{14,6},{15,7},{16,24},{17,... | collective-permute-start | bytes 56 | tf_op jit(solution)/shard_map/ppermute | solution.py:484
  85.2 5.1 %collective-permute-done.17 = f32[2,2,1]{2,1,0:T(2,128)S(1)} collective-permute-done((f32[2,2,1]{2,1,0:T(2,128)S(1)}, f32[2,2,1]{2,1,0:T(2,128)S(1)}, u32[]{:S(2)}, u32[]{:S(2)}) %collective-permute-start.17) | collective-permute-done | bytes 48 | tf_op jit(solution)/shard_map/ppermute | solution.py:484
  90.3 0.7 copy.8
  (6 shorter events, 0.0 us)
Async XLA Ops:
  0.7 23.1 %copy-start.3 = (s32[1,4,6,2]{2,3,1,0:T(2,128)S(1)}, s32[1,4,6,2]{2,3,1,0:T(2,128)}, u32[]{:S(2)}) copy-start(s32[1,4,6,2]{2,3,1,0:T(2,128)} %param.10) | copy-start | bytes 580
  1.9 21.3 %collective-permute-start.7 = (bf16[2,6,2,128,128]{4,3,2,1,0:T(8,128)(2,1)S(1)}, bf16[2,6,2,128,128]{4,3,2,1,0:T(8,128)(2,1)S(1)}, u32[]{:S(2)}, u32[]{:S(2)}) collective-permute-start(bf16[2,6,2,128,128]{4,3,2,1,0:T(8,128)(2,1)S(1)} %pick_source.1.refs_9_.refs_10_), channel_id=1, source_target_pairs={{8,0},{10,2},{4,12},{6,14},{9,1},{11,3},{5,13},{7,15},{24,16},{26,... | collective-permute-start | bytes 2359304 | tf_op jit(solution)/shard_map/ppermute | solution.py:401
  23.2 14.3 %collective-permute-start.8 = (bf16[2,6,2,128,128]{4,3,2,1,0:T(8,128)(2,1)S(1)}, bf16[2,6,2,128,128]{4,3,2,1,0:T(8,128)(2,1)S(1)}, u32[]{:S(2)}, u32[]{:S(2)}) collective-permute-start(bf16[2,6,2,128,128]{4,3,2,1,0:T(8,128)(2,1)S(1)} %collective-permute-done.7.refs_8_.refs_0_), channel_id=1, source_target_pairs={{0,1},{1,0},{2,3},{3,2},{4,5},{5,4},{6,7},{7,6},{8,9},{9,8},{10,11... | collective-permute-start | bytes 2359304 | tf_op jit(solution)/shard_map/ppermute | solution.py:400
  23.2 6.4 %collective-permute-start.6 = (s32[1]{0:T(128)}, s32[1]{0:T(128)}, u32[]{:S(2)}, u32[]{:S(2)}) collective-permute-start(s32[1]{0:T(128)} %param.11), channel_id=1, source_target_pairs={{0,1},{1,0},{2,3},{3,2},{4,5},{5,4},{6,7},{7,6},{8,9},{9,8},{10,11... | collective-permute-start | bytes 20 | tf_op jit(solution)/shard_map/ppermute | solution.py:400
  23.9 15.7 %collective-permute-start.12 = (s32[48]{0:T(128)S(1)}, s32[48]{0:T(128)S(1)}, u32[]{:S(2)}, u32[]{:S(2)}) collective-permute-start(s32[48]{0:T(128)S(1)} %reshape.10.refs_5_.refs_7_), channel_id=1, source_target_pairs={{0,1},{1,0},{2,3},{3,2},{4,5},{5,4},{6,7},{7,6},{8,9},{9,8},{10,11... | collective-permute-start | bytes 584 | tf_op jit(solution)/shard_map/ppermute | solution.py:400
  24.0 13.4 %collective-permute-start.10 = (s32[48]{0:T(128)S(1)}, s32[48]{0:T(128)S(1)}, u32[]{:S(2)}, u32[]{:S(2)}) collective-permute-start(s32[48]{0:T(128)S(1)} %reshape.10.refs_5_.refs_7_), channel_id=1, source_target_pairs={{8,0},{10,2},{4,12},{6,14},{9,1},{11,3},{5,13},{7,15},{24,16},{26,... | collective-permute-start | bytes 584 | tf_op jit(solution)/shard_map/ppermute | solution.py:401
  29.3 20.5 %collective-permute-start.13 = (bf16[2,6,2,128,128]{4,3,2,1,0:T(8,128)(2,1)S(1)}, bf16[2,6,2,128,128]{4,3,2,1,0:T(8,128)(2,1)S(1)}, u32[]{:S(2)}, u32[]{:S(2)}) collective-permute-start(bf16[2,6,2,128,128]{4,3,2,1,0:T(8,128)(2,1)S(1)} %pick_source.1.refs_9_.refs_10_), channel_id=1, source_target_pairs={{0,1},{1,0},{2,3},{3,2},{4,5},{5,4},{6,7},{7,6},{8,9},{9,8},{10,11... | collective-permute-start | bytes 2359304 | tf_op jit(solution)/shard_map/ppermute | solution.py:400
  31.6 0.7 copy-start
  32.2 9.4 %copy-start.1 = (s32[8]{0:T(128)S(1)}, s32[8]{0:T(128)}, u32[]{:S(2)}) copy-start(s32[8]{0:T(128)} %get-tuple-element.109.refs_1_) | copy-start | bytes 100
  35.2 26.5 %collective-permute-start.14 = (bf16[2,6,2,128,128]{4,3,2,1,0:T(8,128)(2,1)S(1)}, bf16[2,6,2,128,128]{4,3,2,1,0:T(8,128)(2,1)S(1)}, u32[]{:S(2)}, u32[]{:S(2)}) collective-permute-start(bf16[2,6,2,128,128]{4,3,2,1,0:T(8,128)(2,1)S(1)} %get-tuple-element.112.refs_11_), channel_id=1, source_target_pairs={{8,0},{10,2},{4,12},{6,14},{9,1},{11,3},{5,13},{7,15},{24,16},{26,... | collective-permute-start | bytes 2359304 | tf_op jit(solution)/shard_map/ppermute | solution.py:401
  37.5 12.4 %collective-permute-start.11 = (s32[48]{0:T(128)S(1)}, s32[48]{0:T(128)S(1)}, u32[]{:S(2)}, u32[]{:S(2)}) collective-permute-start(s32[48]{0:T(128)S(1)} %collective-permute-done.10.refs_4_.refs_6_), channel_id=1, source_target_pairs={{0,1},{1,0},{2,3},{3,2},{4,5},{5,4},{6,7},{7,6},{8,9},{9,8},{10,11... | collective-permute-start | bytes 584 | tf_op jit(solution)/shard_map/ppermute | solution.py:400
  37.5 42.6 %collective-permute-start.15 = (bf16[2,3,2,128,128]{4,3,2,1,0:T(8,128)(2,1)}, bf16[2,3,2,128,128]{4,3,2,1,0:T(8,128)(2,1)}, u32[]{:S(2)}, u32[]{:S(2)}) collective-permute-start(bf16[2,3,2,128,128]{4,3,2,1,0:T(8,128)(2,1)} %get-tuple-element.123.refs_12_), channel_id=1, source_target_pairs={{8,0},{10,2},{4,12},{6,14},{9,1},{11,3},{5,13},{7,15},{24,16},{26,... | collective-permute-start | bytes 1179656 | tf_op jit(solution)/shard_map/ppermute | solution.py:401
  39.6 41.8 %collective-permute-start.9 = (bf16[2,3,2,128,128]{4,3,2,1,0:T(8,128)(2,1)S(1)}, bf16[2,3,2,128,128]{4,3,2,1,0:T(8,128)(2,1)}, u32[]{:S(2)}, u32[]{:S(2)}) collective-permute-start(bf16[2,3,2,128,128]{4,3,2,1,0:T(8,128)(2,1)S(1)} %get-tuple-element.107.refs_13_), channel_id=1, source_target_pairs={{8,0},{10,2},{4,12},{6,14},{9,1},{11,3},{5,13},{7,15},{24,16},{26,... | collective-permute-start | bytes 1179656 | tf_op jit(solution)/shard_map/ppermute | solution.py:401
  49.8 11.4 %copy-start.2 = (f32[4,8,128]{2,1,0:T(8,128)S(1)}, f32[4,8,128]{2,1,0:T(8,128)}, u32[]{:S(2)}) copy-start(f32[4,8,128]{2,1,0:T(8,128)} %get-tuple-element.116.refs_3_) | copy-start | bytes 49156
  62.9 12.2 %collective-permute-start.1 = (bf16[2,3,2,128,128]{4,3,2,1,0:T(8,128)(2,1)S(1)}, bf16[2,3,2,128,128]{4,3,2,1,0:T(8,128)(2,1)S(1)}, u32[]{:S(2)}, u32[]{:S(2)}) collective-permute-start(bf16[2,3,2,128,128]{4,3,2,1,0:T(8,128)(2,1)S(1)} %get-tuple-element.60), channel_id=1, source_target_pairs={{8,0},{10,2},{4,12},{6,14},{24,16},{26,18},{20,28},{22,30}} | collective-permute-start | bytes 1179656 | tf_op jit(solution)/shard_map/cond/branch_1_fun/ppermute | solution.py:467
  64.2 15.1 %collective-permute-start = (bf16[2,3,2,128,128]{4,3,2,1,0:T(8,128)(2,1)S(1)}, bf16[2,3,2,128,128]{4,3,2,1,0:T(8,128)(2,1)S(1)}, u32[]{:S(2)}, u32[]{:S(2)}) collective-permute-start(bf16[2,3,2,128,128]{4,3,2,1,0:T(8,128)(2,1)S(1)} %get-tuple-element.56), channel_id=1, source_target_pairs={{8,0},{10,2},{4,12},{6,14},{24,16},{26,18},{20,28},{22,30}} | collective-permute-start | bytes 1179656 | tf_op jit(solution)/shard_map/cond/branch_1_fun/ppermute | solution.py:467
  82.8 1.2 %collective-permute-start.16 = (f32[2,2,1]{2,1,0:T(2,128)S(1)}, f32[2,2,1]{2,1,0:T(2,128)S(1)}, u32[]{:S(2)}, u32[]{:S(2)}) collective-permute-start(f32[2,2,1]{2,1,0:T(2,128)S(1)} %get-tuple-element.126), channel_id=1, source_target_pairs={{0,1},{1,0},{2,3},{3,2},{4,5},{5,4},{6,7},{7,6},{8,9},{9,8},{10,11... | collective-permute-start | bytes 56 | tf_op jit(solution)/shard_map/ppermute | solution.py:400
  83.9 6.4 %collective-permute-start.17 = (f32[2,2,1]{2,1,0:T(2,128)S(1)}, f32[2,2,1]{2,1,0:T(2,128)S(1)}, u32[]{:S(2)}, u32[]{:S(2)}) collective-permute-start(f32[2,2,1]{2,1,0:T(2,128)S(1)} %add.6), channel_id=1, source_target_pairs={{0,8},{1,9},{2,10},{3,11},{12,4},{13,5},{14,6},{15,7},{16,24},{17,... | collective-permute-start | bytes 56 | tf_op jit(solution)/shard_map/ppermute | solution.py:484

commit v3 on v1

--- a/solution.py
+++ b/solution.py
@@ -23,22 +23,32 @@
     return pl.CostEstimate(flops=flops, bytes_accessed=size, transcendentals=0)
 
 
-def pick_source_kernel(source_ref, fields_ref, out_ref, sems):
-    time = lax.rem(source_ref[0], I32(fields_ref.shape[0]))
-    copies = [
-        pltpu.make_async_copy(fields_ref.at[time, part, r], out_ref.at[part, r], sems.at[part, r])
-        for part in range(fields_ref.shape[1])
-        for r in range(fields_ref.shape[2])
-    ]
-    for copy in copies:
-        copy.start()
-    for copy in copies:
-        copy.wait()
-
-
-def pick_source(source, fields):
-    return pl.pallas_call(
-        pick_source_kernel,
+def pick_source_kernel(senders, source_ref, fields_ref, out_ref, sems):
+    first, last = senders
+    group = lax.axis_index("mom")
+    sends = (group >= first) & (group < last)
+
+    @pl.when(sends)
+    def _():
+        time = lax.rem(source_ref[0], I32(fields_ref.shape[0]))
+        copies = [
+            pltpu.make_async_copy(fields_ref.at[time, part, r], out_ref.at[part, r], sems.at[part, r])
+            for part in range(fields_ref.shape[1])
+            for r in range(fields_ref.shape[2])
+        ]
+        for copy in copies:
+            copy.start()
+        for copy in copies:
+            copy.wait()
+
+    @pl.when(jnp.logical_not(sends))
+    def _():
+        out_ref[...] = jnp.zeros_like(out_ref)
+
+
+def pick_source(source, fields, senders):
+    return pl.pallas_call(
+        lambda *refs: pick_source_kernel(senders, *refs),
         out_shape=jax.ShapeDtypeStruct(fields.shape[1:], fields.dtype),
         in_specs=[SMEM, ANY],
         out_specs=VMEM,
@@ -402,8 +412,8 @@
 
     cols = block_cols.reshape(-1)
     far_cols = to_partner(cols)
-    own_field = pick_source(sources, fields)
-    far = [to_partner(own_field)]
+    senders = min(source for source, _ in pairs), max(source for source, _ in pairs) + 1
+    far = [to_partner(pick_source(sources, fields, senders))]
 
     other_time = swap(sources)
     order, active, full, masks = plan(core, sources, other_time, deltas, times)
@@ -411,7 +421,8 @@
     half = rows // 2
     pieces = [(slot, 0, rows) for slot in range(times - 1)]
     pieces += [(times - 1, 0, half), (times - 1, half, rows - half)]
-    picked = [own_field, *pick_others(order, fields, pieces[1:])]
+    picked = pick_others(order, fields, pieces)
+    own_field = picked[0]
     *early, near, late_low, late_high = picked
     far += [to_partner(field) for field in early[1:]]
     near, far[0] = lax.optimization_barrier((near, far[0]))

time: 84.4 us -> 65 us (0.77)
  waiting for transfers between devices: 36.5 us -> 24.8 us
  starting transfers between devices: 18.2 us -> 13.8 us
  Pallas kernels: 26.2 us -> 23.1 us
    ppermute x2 -> x0, waiting for transfers between devices: 21.3 us -> none  [the longest x1 14.3 us: branch(): lax.ppermute(low, both, routes)]
    ppermute x4, waiting for transfers between devices: 9 us -> 18.6 us  [local(): to_partner = lambda value: lax.ppermute(value, 'mom', pairs)]
    ppermute x2 -> x0, starting transfers between devices: 2.63 us -> none  [the longest x1 1.31 us: branch(): lax.ppermute(low, both, routes)]
    ppermute x4, starting transfers between devices: 13.4 us -> 11.5 us  [local(): to_partner = lambda value: lax.ppermute(value, 'mom', pairs)]
    pallas_call x2, Pallas kernels: 17.2 us -> 15.4 us  [weights(): pl.pallas_call(lambda *refs: weights_kernel(s, pieces, *refs), out_shape=...]
    pallas_call x1, Pallas kernels: 1.71 us -> 0.55 us  [last(): pl.pallas_call(last_kernel, out_shape=[jax.ShapeDtypeStruct((2, share, 1)...]
  transfers between devices with their start and end apart: 13 -> 11, of which waited for: 5 -> 4; matrix products, arithmetic and copies ran while one was open for 0% -> 0% of each run, Pallas kernels for 28% -> 33%
where the time goes in v3:
time: 65 us; the launch traced here: 64.7 us
  waiting for transfers between devices  24.8 us (38%)
  Pallas kernels  23.1 us (36%)
  starting transfers between devices  13.8 us (21%)
  local copies, waits for them, and re-layouts  1.5 us (2%)
  between operations  1.41 us (2%)
    ppermute x4, waiting for transfers between devices, local(): to_partner = lambda value: lax.ppermute(value, 'mom', pairs)  18.6 us
    pallas_call x2, Pallas kernels, weights(): pl.pallas_call(lambda *refs: weights_kernel(s, pieces, *refs), out_shape=...  15.4 us
    ppermute x4, starting transfers between devices, local(): to_partner = lambda value: lax.ppermute(value, 'mom', pairs)  11.5 us
    ppermute x1, waiting for transfers between devices, local(): return total + lax.ppermute(total, both, back)  5.08 us
    pallas_call x1, Pallas kernels, pick_others(): pl.pallas_call(lambda *refs: pick_kernel(pieces, *refs), out_shape=[jax.S...  2.44 us
    pallas_call x1, Pallas kernels, plan(): pl.pallas_call(plan_kernel, out_shape=[jax.ShapeDtypeStruct((times,), I32...  1.98 us
  transfers between devices with their start and end apart: 11, of which 4 were waited for; matrix products, arithmetic and copies ran while one was open for 0% of the time, Pallas kernels for 33%

profile of v3, /device:TPU:8, one launch (start us, length us, event | category | flops | bytes accessed | tf_op | source)
XLA Modules:
  0.0 64.7 jit_solution(3922523783783396092)
XLA Ops:
  0.7 0.0 copy-start.2
  0.7 1.3 %pick_source.1 = bf16[2,6,2,128,128]{4,3,2,1,0:T(8,128)(2,1)S(1)} custom-call(s32[1]{0:T(128)S(6)} %copy.25.own_ref.refs_0_.refs_2_.refs_3_, bf16[4,2,6,2,128,128]{5,4,3,2,1,0:T(8,128)(2,1)} %bitcast.3), custom_call_target="tpu_custom_call" | custom-call | bytes 1600000 | tf_op jit(solution)/shard_map/pick_source/pallas_call | solution.py:50
  1.9 3.5 %collective-permute-start.7 = (bf16[2,6,2,128,128]{4,3,2,1,0:T(8,128)(2,1)S(1)}, bf16[2,6,2,128,128]{4,3,2,1,0:T(8,128)(2,1)S(1)}, u32[]{:S(2)}, u32[]{:S(2)}) collective-permute-start(bf16[2,6,2,128,128]{4,3,2,1,0:T(8,128)(2,1)S(1)} %pick_source.1), channel_id=1, source_target_pairs={{8,0},{10,2},{4,12},{6,14},{9,1},{11,3},{5,13},{7,15},{24,16},{26,... | collective-permute-start | bytes 2359304 | tf_op jit(solution)/shard_map/ppermute | solution.py:411
  5.5 0.1 collective-permute-start.6
  5.5 0.0 copy-done.2
  5.6 0.1 copy.7
  5.7 0.1 reshape.10.refs_5_.refs_7_
  5.8 0.6 collective-permute-start.11
  6.3 1.3 %collective-permute-start.9 = (s32[48]{0:T(128)S(1)}, s32[48]{0:T(128)S(1)}, u32[]{:S(2)}, u32[]{:S(2)}) collective-permute-start(s32[48]{0:T(128)S(1)} %reshape.10.refs_5_.refs_7_), channel_id=1, source_target_pairs={{8,0},{10,2},{4,12},{6,14},{9,1},{11,3},{5,13},{7,15},{24,16},{26,... | collective-permute-start | bytes 584 | tf_op jit(solution)/shard_map/ppermute | solution.py:411
  7.6 0.0 collective-permute-done.6.other_ref.refs_2_.refs_3_
  7.6 2.0 %plan.1 = (s32[4]{0:T(128)}, s32[8]{0:T(128)}, s32[1]{0:T(128)}, f32[4,8,128]{2,1,0:T(8,128)S(1)}) custom-call(s32[1]{0:T(128)} %bitcast.core_ref, s32[1]{0:T(128)S(6)} %copy.25.own_ref.refs_0_.refs_2_.refs_3_, s32[1]{0:T(128)} %collective-permute-done.6.other_ref.refs_2_.refs_3_, s32[4]{0:T(128)} %deltas_ref.1), custom_call_target="tpu_custom_call" | custom-call | bytes 1000 | tf_op jit(solution)/shard_map/plan/pallas_call | solution.py:140
  9.6 0.0 copy-start
  9.6 0.6 copy-done
  10.2 0.0 copy-start.1
  10.2 2.4 %pick_others.1 = (bf16[2,6,2,128,128]{4,3,2,1,0:T(8,128)(2,1)S(1)}, bf16[2,6,2,128,128]{4,3,2,1,0:T(8,128)(2,1)S(1)}, bf16[2,6,2,128,128]{4,3,2,1,0:T(8,128)(2,1...) custom-call(s32[4]{0:T(128)S(1)} %copy-done, bf16[4,2,6,2,128,128]{5,4,3,2,1,0:T(8,128)(2,1)} %bitcast.4), custom_call_target="tpu_custom_call" | custom-call | bytes 5000000 | tf_op jit(solution)/shard_map/pick_others/pallas_call | solution.py:78
  12.7 0.1 collective-permute-start.13
  12.8 1.3 %collective-permute-start.14 = (bf16[2,6,2,128,128]{4,3,2,1,0:T(8,128)(2,1)S(1)}, bf16[2,6,2,128,128]{4,3,2,1,0:T(8,128)(2,1)S(1)}, u32[]{:S(2)}, u32[]{:S(2)}) collective-permute-start(bf16[2,6,2,128,128]{4,3,2,1,0:T(8,128)(2,1)S(1)} %get-tuple-element.110.refs_11_), channel_id=1, source_target_pairs={{8,0},{10,2},{4,12},{6,14},{9,1},{11,3},{5,13},{7,15},{24,16},{26,... | collective-permute-start | bytes 2359304 | tf_op jit(solution)/shard_map/ppermute | solution.py:411
  14.7 8.7 %collective-permute-done.9.refs_4_.refs_6_ = s32[48]{0:T(128)S(1)} collective-permute-done((s32[48]{0:T(128)S(1)}, s32[48]{0:T(128)S(1)}, u32[]{:S(2)}, u32[]{:S(2)}) %collective-permute-start.9) | collective-permute-done | bytes 224 | tf_op jit(solution)/shard_map/ppermute | solution.py:411
  23.4 0.0 collective-permute-start.10
  23.4 0.0 collective-permute-done.7.refs_8_.refs_0_
  23.4 5.3 %collective-permute-start.8 = (bf16[2,6,2,128,128]{4,3,2,1,0:T(8,128)(2,1)S(1)}, bf16[2,6,2,128,128]{4,3,2,1,0:T(8,128)(2,1)S(1)}, u32[]{:S(2)}, u32[]{:S(2)}) collective-permute-start(bf16[2,6,2,128,128]{4,3,2,1,0:T(8,128)(2,1)S(1)} %get-tuple-element.105.refs_12_), channel_id=1, source_target_pairs={{8,0},{10,2},{4,12},{6,14},{9,1},{11,3},{5,13},{7,15},{24,16},{26,... | collective-permute-start | bytes 2359304 | tf_op jit(solution)/shard_map/ppermute | solution.py:411
  28.8 0.0 collective-permute-done.11.refs_5_
  28.8 0.3 collective-permute-start.12
  29.1 0.0 copy-done.1
  29.1 8.0 %weights.2.refs_1_ = f32[4,6,2,2,128,128]{5,4,3,2,1,0:T(8,128)S(1)} custom-call(s32[4]{0:T(128)S(1)} %copy-done, s32[8]{0:T(128)S(1)} %copy-done.1, s32[1]{0:T(128)S(6)} %copy.25.own_ref.refs_0_.refs_2_.refs_3_, s32[1]{0:T(128)S(6)} %copy.25.own_ref.refs_0_.refs_2_.refs_3_, s32[48]{0:T(128)S(1)} %collective-permute-done.9.refs_4_.refs_6_, ...), custom_call_target="tpu_custom_call" | custom-call | flops 80000000000 | bytes 4000000 | tf_op jit(solution)/shard_map/weights/pallas_call | solution.py:272
  37.0 0.0 collective-permute-done.10.refs_4_
  37.0 0.0 collective-permute-done.13.refs_9_
  37.0 0.0 collective-permute-done.12.refs_8_
  37.0 7.5 %weights.3.refs_2_ = f32[4,6,2,2,128,128]{5,4,3,2,1,0:T(8,128)S(1)} custom-call(s32[4]{0:T(128)S(1)} %copy-done, s32[8]{0:T(128)S(1)} %copy-done.1, s32[1]{0:T(128)} %collective-permute-done.6.other_ref.refs_2_.refs_3_, s32[1]{0:T(128)} %collective-permute-done.6.other_ref.refs_2_.refs_3_, s32[48]{0:T(128)S(1)} %collective-permute-done.10.refs_4_, ...), custom_call_target="tpu_custom_call" | custom-call | flops 2000000000 | bytes 4000000 | tf_op jit(solution)/shard_map/weights/pallas_call | solution.py:272
  44.5 0.5 inner.14.refs_4_
  45.1 0.0 collective-permute-done.14.refs_0_
  45.1 0.5 inner.15
  45.6 0.4 conditional.1
  45.6 0.4 stage.4
  46.0 9.9 %collective-permute-done.8.field_ref = bf16[2,6,2,128,128]{4,3,2,1,0:T(8,128)(2,1)S(1)} collective-permute-done((bf16[2,6,2,128,128]{4,3,2,1,0:T(8,128)(2,1)S(1)}, bf16[2,6,2,128,128]{4,3,2,1,0:T(8,128)(2,1)S(1)}, u32[]{:S(2)}, u32[]{:S(2)}) %collective-permute-start.8) | collective-permute-done | bytes 786464 | tf_op jit(solution)/shard_map/ppermute | solution.py:411
  55.9 0.5 last.1
  56.5 0.0 collective-permute-start.15
  56.5 1.1 %collective-permute-done.15 = f32[2,2,1]{2,1,0:T(2,128)S(1)} collective-permute-done((f32[2,2,1]{2,1,0:T(2,128)S(1)}, f32[2,2,1]{2,1,0:T(2,128)S(1)}, u32[]{:S(2)}, u32[]{:S(2)}) %collective-permute-start.15) | collective-permute-done | bytes 48 | tf_op jit(solution)/shard_map/ppermute | solution.py:410
  57.6 1.3 %collective-permute-start.16 = (f32[2,2,1]{2,1,0:T(2,128)S(1)}, f32[2,2,1]{2,1,0:T(2,128)S(1)}, u32[]{:S(2)}, u32[]{:S(2)}) collective-permute-start(f32[2,2,1]{2,1,0:T(2,128)S(1)} %add.6), channel_id=1, source_target_pairs={{0,8},{1,9},{2,10},{3,11},{12,4},{13,5},{14,6},{15,7},{16,24},{17,... | collective-permute-start | bytes 56 | tf_op jit(solution)/shard_map/ppermute | solution.py:493
  58.9 5.1 %collective-permute-done.16 = f32[2,2,1]{2,1,0:T(2,128)S(1)} collective-permute-done((f32[2,2,1]{2,1,0:T(2,128)S(1)}, f32[2,2,1]{2,1,0:T(2,128)S(1)}, u32[]{:S(2)}, u32[]{:S(2)}) %collective-permute-start.16) | collective-permute-done | bytes 48 | tf_op jit(solution)/shard_map/ppermute | solution.py:493
  64.0 0.7 %copy.8 = f32[2,2,1]{1,2,0:T(1,128)} copy(f32[2,2,1]{2,1,0:T(2,128)S(1)} %add.7) | data formatting | bytes 32 | tf_op jit(solution)/shard_map/add | solution.py:493
  (2 shorter events, 0.0 us)
Async XLA Ops:
  0.7 4.9 %copy-start.2 = (s32[1,4,6,2]{2,3,1,0:T(2,128)S(1)}, s32[1,4,6,2]{2,3,1,0:T(2,128)}, u32[]{:S(2)}) copy-start(s32[1,4,6,2]{2,3,1,0:T(2,128)} %param.10) | copy-start | bytes 580
  1.9 21.5 %collective-permute-start.7 = (bf16[2,6,2,128,128]{4,3,2,1,0:T(8,128)(2,1)S(1)}, bf16[2,6,2,128,128]{4,3,2,1,0:T(8,128)(2,1)S(1)}, u32[]{:S(2)}, u32[]{:S(2)}) collective-permute-start(bf16[2,6,2,128,128]{4,3,2,1,0:T(8,128)(2,1)S(1)} %pick_source.1), channel_id=1, source_target_pairs={{8,0},{10,2},{4,12},{6,14},{9,1},{11,3},{5,13},{7,15},{24,16},{26,... | collective-permute-start | bytes 2359304 | tf_op jit(solution)/shard_map/ppermute | solution.py:411
  5.5 2.1 %collective-permute-start.6 = (s32[1]{0:T(128)}, s32[1]{0:T(128)}, u32[]{:S(2)}, u32[]{:S(2)}) collective-permute-start(s32[1]{0:T(128)} %param.11), channel_id=1, source_target_pairs={{0,1},{1,0},{2,3},{3,2},{4,5},{5,4},{6,7},{7,6},{8,9},{9,8},{10,11... | collective-permute-start | bytes 20 | tf_op jit(solution)/shard_map/ppermute | solution.py:410
  5.8 23.0 %collective-permute-start.11 = (s32[48]{0:T(128)S(1)}, s32[48]{0:T(128)S(1)}, u32[]{:S(2)}, u32[]{:S(2)}) collective-permute-start(s32[48]{0:T(128)S(1)} %reshape.10.refs_5_.refs_7_), channel_id=1, source_target_pairs={{0,1},{1,0},{2,3},{3,2},{4,5},{5,4},{6,7},{7,6},{8,9},{9,8},{10,11... | collective-permute-start | bytes 584 | tf_op jit(solution)/shard_map/ppermute | solution.py:410
  6.3 17.1 %collective-permute-start.9 = (s32[48]{0:T(128)S(1)}, s32[48]{0:T(128)S(1)}, u32[]{:S(2)}, u32[]{:S(2)}) collective-permute-start(s32[48]{0:T(128)S(1)} %reshape.10.refs_5_.refs_7_), channel_id=1, source_target_pairs={{8,0},{10,2},{4,12},{6,14},{9,1},{11,3},{5,13},{7,15},{24,16},{26,... | collective-permute-start | bytes 584 | tf_op jit(solution)/shard_map/ppermute | solution.py:411
  9.6 0.6 copy-start
  10.2 18.8 %copy-start.1 = (s32[8]{0:T(128)S(1)}, s32[8]{0:T(128)}, u32[]{:S(2)}) copy-start(s32[8]{0:T(128)} %get-tuple-element.107.refs_1_) | copy-start | bytes 100
  12.7 24.3 %collective-permute-start.13 = (bf16[2,6,2,128,128]{4,3,2,1,0:T(8,128)(2,1)S(1)}, bf16[2,6,2,128,128]{4,3,2,1,0:T(8,128)(2,1)S(1)}, u32[]{:S(2)}, u32[]{:S(2)}) collective-permute-start(bf16[2,6,2,128,128]{4,3,2,1,0:T(8,128)(2,1)S(1)} %get-tuple-element.109.refs_9_.refs_10_), channel_id=1, source_target_pairs={{0,1},{1,0},{2,3},{3,2},{4,5},{5,4},{6,7},{7,6},{8,9},{9,8},{10,11... | collective-permute-start | bytes 2359304 | tf_op jit(solution)/shard_map/ppermute | solution.py:410
  12.8 32.3 %collective-permute-start.14 = (bf16[2,6,2,128,128]{4,3,2,1,0:T(8,128)(2,1)S(1)}, bf16[2,6,2,128,128]{4,3,2,1,0:T(8,128)(2,1)S(1)}, u32[]{:S(2)}, u32[]{:S(2)}) collective-permute-start(bf16[2,6,2,128,128]{4,3,2,1,0:T(8,128)(2,1)S(1)} %get-tuple-element.110.refs_11_), channel_id=1, source_target_pairs={{8,0},{10,2},{4,12},{6,14},{9,1},{11,3},{5,13},{7,15},{24,16},{26,... | collective-permute-start | bytes 2359304 | tf_op jit(solution)/shard_map/ppermute | solution.py:411
  23.4 13.6 %collective-permute-start.10 = (s32[48]{0:T(128)S(1)}, s32[48]{0:T(128)S(1)}, u32[]{:S(2)}, u32[]{:S(2)}) collective-permute-start(s32[48]{0:T(128)S(1)} %collective-permute-done.9.refs_4_.refs_6_), channel_id=1, source_target_pairs={{0,1},{1,0},{2,3},{3,2},{4,5},{5,4},{6,7},{7,6},{8,9},{9,8},{10,11... | collective-permute-start | bytes 584 | tf_op jit(solution)/shard_map/ppermute | solution.py:410
  23.4 32.5 %collective-permute-start.8 = (bf16[2,6,2,128,128]{4,3,2,1,0:T(8,128)(2,1)S(1)}, bf16[2,6,2,128,128]{4,3,2,1,0:T(8,128)(2,1)S(1)}, u32[]{:S(2)}, u32[]{:S(2)}) collective-permute-start(bf16[2,6,2,128,128]{4,3,2,1,0:T(8,128)(2,1)S(1)} %get-tuple-element.105.refs_12_), channel_id=1, source_target_pairs={{8,0},{10,2},{4,12},{6,14},{9,1},{11,3},{5,13},{7,15},{24,16},{26,... | collective-permute-start | bytes 2359304 | tf_op jit(solution)/shard_map/ppermute | solution.py:411
  28.8 8.3 %collective-permute-start.12 = (bf16[2,6,2,128,128]{4,3,2,1,0:T(8,128)(2,1)S(1)}, bf16[2,6,2,128,128]{4,3,2,1,0:T(8,128)(2,1)S(1)}, u32[]{:S(2)}, u32[]{:S(2)}) collective-permute-start(bf16[2,6,2,128,128]{4,3,2,1,0:T(8,128)(2,1)S(1)} %collective-permute-done.7.refs_8_.refs_0_), channel_id=1, source_target_pairs={{0,1},{1,0},{2,3},{3,2},{4,5},{5,4},{6,7},{7,6},{8,9},{9,8},{10,11... | collective-permute-start | bytes 2359304 | tf_op jit(solution)/shard_map/ppermute | solution.py:410
  56.5 1.2 %collective-permute-start.15 = (f32[2,2,1]{2,1,0:T(2,128)S(1)}, f32[2,2,1]{2,1,0:T(2,128)S(1)}, u32[]{:S(2)}, u32[]{:S(2)}) collective-permute-start(f32[2,2,1]{2,1,0:T(2,128)S(1)} %get-tuple-element.122), channel_id=1, source_target_pairs={{0,1},{1,0},{2,3},{3,2},{4,5},{5,4},{6,7},{7,6},{8,9},{9,8},{10,11... | collective-permute-start | bytes 56 | tf_op jit(solution)/shard_map/ppermute | solution.py:410
  57.6 6.4 %collective-permute-start.16 = (f32[2,2,1]{2,1,0:T(2,128)S(1)}, f32[2,2,1]{2,1,0:T(2,128)S(1)}, u32[]{:S(2)}, u32[]{:S(2)}) collective-permute-start(f32[2,2,1]{2,1,0:T(2,128)S(1)} %add.6), channel_id=1, source_target_pairs={{0,8},{1,9},{2,10},{3,11},{12,4},{13,5},{14,6},{15,7},{16,24},{17,... | collective-permute-start | bytes 56 | tf_op jit(solution)/shard_map/ppermute | solution.py:493

commit v4 on v3

--- a/solution.py
+++ b/solution.py
@@ -23,7 +23,8 @@
     return pl.CostEstimate(flops=flops, bytes_accessed=size, transcendentals=0)
 
 
-def pick_source_kernel(senders, source_ref, fields_ref, out_ref, sems):
+def pick_source_kernel(senders, halves, source_ref, fields_ref, *refs):
+    *out_refs, sems = refs
     first, last = senders
     group = lax.axis_index("mom")
     sends = (group >= first) & (group < last)
@@ -32,9 +33,12 @@
     def _():
         time = lax.rem(source_ref[0], I32(fields_ref.shape[0]))
         copies = [
-            pltpu.make_async_copy(fields_ref.at[time, part, r], out_ref.at[part, r], sems.at[part, r])
+            pltpu.make_async_copy(
+                fields_ref.at[time, part, first + r], out_ref.at[part, r], sems.at[part, first + r]
+            )
             for part in range(fields_ref.shape[1])
-            for r in range(fields_ref.shape[2])
+            for (first, rows), out_ref in zip(halves, out_refs)
+            for r in range(rows)
         ]
         for copy in copies:
             copy.start()
@@ -43,15 +47,18 @@
 
     @pl.when(jnp.logical_not(sends))
     def _():
-        out_ref[...] = jnp.zeros_like(out_ref)
-
-
-def pick_source(source, fields, senders):
-    return pl.pallas_call(
-        lambda *refs: pick_source_kernel(senders, *refs),
-        out_shape=jax.ShapeDtypeStruct(fields.shape[1:], fields.dtype),
+        for out_ref in out_refs:
+            out_ref[...] = jnp.zeros_like(out_ref)
+
+
+def pick_source(source, fields, senders, halves):
+    return pl.pallas_call(
+        lambda *refs: pick_source_kernel(senders, halves, *refs),
+        out_shape=[
+            jax.ShapeDtypeStruct((2, rows) + fields.shape[3:], fields.dtype) for _, rows in halves
+        ],
         in_specs=[SMEM, ANY],
-        out_specs=VMEM,
+        out_specs=[VMEM] * len(halves),
         scratch_shapes=[pltpu.SemaphoreType.DMA(fields.shape[1:3])],
         cost_estimate=cost(0, 1_600_000),
         compiler_params=pltpu.CompilerParams(vmem_limit_bytes=52 * 2**20),
@@ -153,10 +160,10 @@
 
 
 def weights_kernel(s, pieces, order_ref, active_ref, *refs):
-    far_ref, own_ref, far_cols, own_cols, m_cols, b_cols, a_ref, d_ref, *refs = refs
+    far_ref, own_ref, far_cols, own_cols, m_cols, b_cols, a_low, a_high, d_ref, *refs = refs
     *b_refs, u_ref, la, ld, bs, yn, held, sems = refs
     slot = pl.program_id(0)
-    rows, per_row, size = a_ref.shape[1], a_ref.shape[2], a_ref.shape[3]
+    rows, per_row, size = d_ref.shape[1], d_ref.shape[2], d_ref.shape[3]
     times = order_ref.shape[0]
     step = rows * per_row
     base = order_ref[slot] * step
@@ -176,7 +183,8 @@
             copy.start()
         for r in range(rows):
             for j in range(per_row):
-                real, imag = a_ref[0, r, j], a_ref[1, r, j]
+                a_ref, at = (a_low, r) if r < a_low.shape[1] else (a_high, r - a_low.shape[1])
+                real, imag = a_ref[0, at, j], a_ref[1, at, j]
                 la[r, j, lo, lo] = real
                 la[r, j, lo, hi] = -imag
                 la[r, j, hi, lo] = imag
@@ -267,7 +275,7 @@
 
 def weights(flops, s, pieces, order, active, far_time, own_time, far_cols, own_cols, m_cols, b_cols, a, d, picked):
     times = order.shape[0]
-    _, rows, per_row, size, _ = a.shape
+    _, rows, per_row, size, _ = d.shape
     whole = lambda slot, *_: (0, 0, 0, 0, 0)
     return pl.pallas_call(
         lambda *refs: weights_kernel(s, pieces, *refs),
@@ -276,8 +284,8 @@
             num_scalar_prefetch=8,
             grid=(times,),
             in_specs=[
-                pl.BlockSpec(a.shape, whole),
-                pl.BlockSpec(a.shape, whole),
+                *[pl.BlockSpec(half.shape, whole) for half in a],
+                pl.BlockSpec(d.shape, whole),
                 *[ANY] * len(picked),
             ],
             out_specs=pl.BlockSpec(
@@ -288,14 +296,14 @@
                 pltpu.VMEM((rows, per_row, 2 * size, 2 * size), BF16),
                 pltpu.VMEM((rows, 2 * size, per_row * size), BF16),
                 pltpu.VMEM((rows, rows * size, 2 * size), BF16),
-                pltpu.VMEM((2,) + a.shape, a.dtype),
+                pltpu.VMEM((2,) + d.shape, d.dtype),
                 pltpu.SemaphoreType.DMA((len(picked), 2)),
             ],
         ),
         compiler_params=pltpu.CompilerParams(vmem_limit_bytes=16 * 2**20),
         cost_estimate=cost(flops, times * 1_000_000),
         name="weights",
-    )(order, active, far_time, own_time, far_cols, own_cols, m_cols, b_cols, a, d, *picked)
+    )(order, active, far_time, own_time, far_cols, own_cols, m_cols, b_cols, *a, d, *picked)
 
 
 def products(field_ref, u_refs, slot, first):
@@ -413,25 +421,26 @@
     cols = block_cols.reshape(-1)
     far_cols = to_partner(cols)
     senders = min(source for source, _ in pairs), max(source for source, _ in pairs) + 1
-    far = [to_partner(pick_source(sources, fields, senders))]
+    rows = fields.shape[2]
+    half = rows // 2
+    halves = [(0, half), (half, rows - half)]
+    far_source = [to_partner(part) for part in pick_source(sources, fields, senders, halves)]
 
     other_time = swap(sources)
     order, active, full, masks = plan(core, sources, other_time, deltas, times)
-    rows = fields.shape[2]
-    half = rows // 2
     pieces = [(slot, 0, rows) for slot in range(times - 1)]
-    pieces += [(times - 1, 0, half), (times - 1, half, rows - half)]
+    pieces += [(times - 1, *part) for part in halves]
     picked = pick_others(order, fields, pieces)
     own_field = picked[0]
     *early, near, late_low, late_high = picked
-    far += [to_partner(field) for field in early[1:]]
-    near, far[0] = lax.optimization_barrier((near, far[0]))
+    far = [to_partner(field) for field in early[1:]]
+    near, far_source = lax.optimization_barrier((near, far_source))
     near = to_partner(near)
 
     other_cols = swap(cols)
     far_other_cols = swap(far_cols)
     other_field = swap(own_field)
-    far_other = swap(far[0])
+    far_other = [swap(part) for part in far_source]
     u0 = weights(
         80_000_000_000,
         0,
@@ -444,7 +453,7 @@
         cols,
         far_cols,
         cols,
-        far[0],
+        far_source,
         own_field,
         picked,
     )
@@ -464,8 +473,9 @@
         other_field,
         picked,
     )
-    lines = inner(0, 0, far[0], u0, u1, masks)
-    for slot, field in enumerate(far[1:], 1):
+    lines = inner(0, 0, far_source[0], u0, u1, masks)
+    lines = inner(0, half, far_source[1], u0, u1, masks, lines)
+    for slot, field in enumerate(far, 1):
         lines = inner(slot, 0, field, u0, u1, masks, lines)
 
     both = ("mom", "src")

time: 65 us -> 78 us (1.20)
  starting transfers between devices: 13.8 us -> 19.4 us
  waiting for transfers between devices: 24.8 us -> 29.7 us
  Pallas kernels: 23.1 us -> 25.6 us
    ppermute x0 -> x2, waiting for transfers between devices: none -> 15.3 us  [the longest x1 11.3 us: branch(): lax.ppermute(low, both, routes)]
    ppermute x4 -> x5, waiting for transfers between devices: 18.6 us -> 7.64 us  [local(): to_partner = lambda value: lax.ppermute(value, 'mom', pairs)]
    ppermute x0 -> x2, starting transfers between devices: none -> 4.01 us  [the longest x1 2.7 us: branch(): lax.ppermute(low, both, routes)]
    pallas_call x2, Pallas kernels: 15.4 us -> 17.3 us  [weights(): pl.pallas_call(lambda *refs: weights_kernel(s, pieces, *refs), out_shape=...]
    ppermute x4 -> x5, starting transfers between devices: 11.5 us -> 12.8 us  [local(): to_partner = lambda value: lax.ppermute(value, 'mom', pairs)]
    pallas_call x2 -> x5, Pallas kernels: 1.05 us -> 1.71 us  [inner(): pl.pallas_call(lambda *refs: inner_kernel(slot, first, *refs), out_shape=...]
    ppermute x6 -> x7, waiting for transfers between devices: 1.16 us -> 1.68 us  [local(): swap = lambda value: lax.ppermute(value, 'src', [(0, 1), (1, 0)])]
  transfers between devices with their start and end apart: 11 -> 15, of which waited for: 4 -> 6; matrix products, arithmetic and copies ran while one was open for 0% -> 0% of each run, Pallas kernels for 33% -> 31%
where the time goes in v4:
time: 78 us; the launch traced here: 77.8 us
  waiting for transfers between devices  29.7 us (38%)
  Pallas kernels  25.6 us (33%)
  starting transfers between devices  19.4 us (25%)
  local copies, waits for them, and re-layouts  1.54 us (2%)
  between operations  1.45 us (2%)
    pallas_call x2, Pallas kernels, weights(): pl.pallas_call(lambda *refs: weights_kernel(s, pieces, *refs), out_shape=...  17.3 us
    ppermute x5, starting transfers between devices, local(): to_partner = lambda value: lax.ppermute(value, 'mom', pairs)  12.8 us
    ppermute x1, waiting for transfers between devices, branch(): lax.ppermute(low, both, routes)  11.3 us
    ppermute x5, waiting for transfers between devices, local(): to_partner = lambda value: lax.ppermute(value, 'mom', pairs)  7.64 us
    ppermute x1, waiting for transfers between devices, local(): return total + lax.ppermute(total, both, back)  5.08 us
    ppermute x1, waiting for transfers between devices, branch(): lax.ppermute(high, both, routes)  3.93 us
    ppermute x1, starting transfers between devices, branch(): lax.ppermute(low, both, routes)  2.7 us
    pallas_call x1, Pallas kernels, pick_others(): pl.pallas_call(lambda *refs: pick_kernel(pieces, *refs), out_shape=[jax.S...  2.44 us
  transfers between devices with their start and end apart: 15, of which 6 were waited for; matrix products, arithmetic and copies ran while one was open for 0% of the time, Pallas kernels for 31%

profile of v4, /device:TPU:8, one launch (start us, length us, event | category | flops | bytes accessed | tf_op | source)
XLA Modules:
  0.0 77.8 jit_solution(9494302120872306447)
XLA Ops:
  0.7 0.0 copy-start.2
  0.7 1.3 %pick_source.1 = (bf16[2,3,2,128,128]{4,3,2,1,0:T(8,128)(2,1)S(1)}, bf16[2,3,2,128,128]{4,3,2,1,0:T(8,128)(2,1)S(1)}) custom-call(s32[1]{0:T(128)S(6)} %copy.25.own_ref.refs_0_.refs_2_.refs_3_, bf16[4,2,6,2,128,128]{5,4,3,2,1,0:T(8,128)(2,1)} %bitcast.3), custom_call_target="tpu_custom_call" | custom-call | bytes 1600000 | tf_op jit(solution)/shard_map/pick_source/pallas_call | solution.py:55
  1.9 3.5 %collective-permute-start.7 = (bf16[2,3,2,128,128]{4,3,2,1,0:T(8,128)(2,1)S(1)}, bf16[2,3,2,128,128]{4,3,2,1,0:T(8,128)(2,1)S(1)}, u32[]{:S(2)}, u32[]{:S(2)}) collective-permute-start(bf16[2,3,2,128,128]{4,3,2,1,0:T(8,128)(2,1)S(1)} %get-tuple-element.108), channel_id=1, source_target_pairs={{8,0},{10,2},{4,12},{6,14},{9,1},{11,3},{5,13},{7,15},{24,16},{26,... | collective-permute-start | bytes 1179656 | tf_op jit(solution)/shard_map/ppermute | solution.py:419
  5.4 1.3 %collective-permute-start.8 = (bf16[2,3,2,128,128]{4,3,2,1,0:T(8,128)(2,1)S(1)}, bf16[2,3,2,128,128]{4,3,2,1,0:T(8,128)(2,1)S(1)}, u32[]{:S(2)}, u32[]{:S(2)}) collective-permute-start(bf16[2,3,2,128,128]{4,3,2,1,0:T(8,128)(2,1)S(1)} %get-tuple-element.109), channel_id=1, source_target_pairs={{8,0},{10,2},{4,12},{6,14},{9,1},{11,3},{5,13},{7,15},{24,16},{26,... | collective-permute-start | bytes 1179656 | tf_op jit(solution)/shard_map/ppermute | solution.py:419
  6.8 0.1 collective-permute-start.6
  6.9 0.1 copy.7
  7.0 0.1 reshape.10.refs_5_.refs_7_
  7.1 0.6 collective-permute-start.12
  7.6 1.3 %collective-permute-start.10 = (s32[48]{0:T(128)S(1)}, s32[48]{0:T(128)S(1)}, u32[]{:S(2)}, u32[]{:S(2)}) collective-permute-start(s32[48]{0:T(128)S(1)} %reshape.10.refs_5_.refs_7_), channel_id=1, source_target_pairs={{8,0},{10,2},{4,12},{6,14},{9,1},{11,3},{5,13},{7,15},{24,16},{26,... | collective-permute-start | bytes 584 | tf_op jit(solution)/shard_map/ppermute | solution.py:419
  8.9 0.0 collective-permute-done.6.other_ref.refs_2_.refs_3_
  8.9 1.9 %plan.1 = (s32[4]{0:T(128)}, s32[8]{0:T(128)}, s32[1]{0:T(128)}, f32[4,8,128]{2,1,0:T(8,128)S(1)}) custom-call(s32[1]{0:T(128)} %bitcast.core_ref, s32[1]{0:T(128)S(6)} %copy.25.own_ref.refs_0_.refs_2_.refs_3_, s32[1]{0:T(128)} %collective-permute-done.6.other_ref.refs_2_.refs_3_, s32[4]{0:T(128)} %deltas_ref.1), custom_call_target="tpu_custom_call" | custom-call | bytes 1000 | tf_op jit(solution)/shard_map/plan/pallas_call | solution.py:147
  10.8 0.7 copy-done
  11.5 2.4 %pick_others.1 = (bf16[2,6,2,128,128]{4,3,2,1,0:T(8,128)(2,1)S(1)}, bf16[2,6,2,128,128]{4,3,2,1,0:T(8,128)(2,1)S(1)}, bf16[2,6,2,128,128]{4,3,2,1,0:T(8,128)(2,1...) custom-call(s32[4]{0:T(128)S(1)} %copy-done, bf16[4,2,6,2,128,128]{5,4,3,2,1,0:T(8,128)(2,1)} %bitcast.4), custom_call_target="tpu_custom_call" | custom-call | bytes 5000000 | tf_op jit(solution)/shard_map/pick_others/pallas_call | solution.py:85
  14.0 0.1 collective-permute-start.15
  14.6 7.6 %collective-permute-done.10.refs_4_.refs_6_ = s32[48]{0:T(128)S(1)} collective-permute-done((s32[48]{0:T(128)S(1)}, s32[48]{0:T(128)S(1)}, u32[]{:S(2)}, u32[]{:S(2)}) %collective-permute-start.10) | collective-permute-done | bytes 224 | tf_op jit(solution)/shard_map/ppermute | solution.py:419
  22.2 5.3 %collective-permute-start.16 = (bf16[2,6,2,128,128]{4,3,2,1,0:T(8,128)(2,1)S(1)}, bf16[2,6,2,128,128]{4,3,2,1,0:T(8,128)(2,1)S(1)}, u32[]{:S(2)}, u32[]{:S(2)}) collective-permute-start(bf16[2,6,2,128,128]{4,3,2,1,0:T(8,128)(2,1)S(1)} %get-tuple-element.116.refs_12_), channel_id=1, source_target_pairs={{8,0},{10,2},{4,12},{6,14},{9,1},{11,3},{5,13},{7,15},{24,16},{26,... | collective-permute-start | bytes 2359304 | tf_op jit(solution)/shard_map/ppermute | solution.py:419
  27.6 0.0 collective-permute-done.7.refs_8_.refs_0_
  27.6 0.1 collective-permute-start.11
  27.7 0.0 collective-permute-done.8.refs_9_.refs_0_
  27.7 0.5 collective-permute-start.13
  28.2 0.0 collective-permute-done.12.refs_5_
  28.2 0.1 collective-permute-start.14
  28.3 0.5 collective-permute-done.11.refs_4_
  28.8 1.3 %collective-permute-start.9 = (bf16[2,6,2,128,128]{4,3,2,1,0:T(8,128)(2,1)S(1)}, bf16[2,6,2,128,128]{4,3,2,1,0:T(8,128)(2,1)S(1)}, u32[]{:S(2)}, u32[]{:S(2)}) collective-permute-start(bf16[2,6,2,128,128]{4,3,2,1,0:T(8,128)(2,1)S(1)} %get-tuple-element.110.refs_13_), channel_id=1, source_target_pairs={{8,0},{10,2},{4,12},{6,14},{9,1},{11,3},{5,13},{7,15},{24,16},{26,... | collective-permute-start | bytes 2359304 | tf_op jit(solution)/shard_map/ppermute | solution.py:419
  30.1 8.1 %weights.2.refs_1_ = f32[4,6,2,2,128,128]{5,4,3,2,1,0:T(8,128)S(1)} custom-call(s32[4]{0:T(128)S(1)} %copy-done, s32[8]{0:T(128)S(1)} %copy-done.1, s32[1]{0:T(128)S(6)} %copy.25.own_ref.refs_0_.refs_2_.refs_3_, s32[1]{0:T(128)S(6)} %copy.25.own_ref.refs_0_.refs_2_.refs_3_, s32[48]{0:T(128)S(1)} %collective-permute-done.10.refs_4_.refs_6_, ...), custom_call_target="tpu_custom_call" | custom-call | flops 80000000000 | bytes 4000000 | tf_op jit(solution)/shard_map/weights/pallas_call | solution.py:280
  38.2 0.0 collective-permute-done.13.refs_8_
  38.2 0.0 collective-permute-done.14.refs_9_
  38.3 0.0 collective-permute-done.15.refs_10_
  38.3 9.3 %weights.3.refs_2_ = f32[4,6,2,2,128,128]{5,4,3,2,1,0:T(8,128)S(1)} custom-call(s32[4]{0:T(128)S(1)} %copy-done, s32[8]{0:T(128)S(1)} %copy-done.1, s32[1]{0:T(128)} %collective-permute-done.6.other_ref.refs_2_.refs_3_, s32[1]{0:T(128)} %collective-permute-done.6.other_ref.refs_2_.refs_3_, s32[48]{0:T(128)S(1)} %collective-permute-done.11.refs_4_, ...), custom_call_target="tpu_custom_call" | custom-call | flops 2000000000 | bytes 4000000 | tf_op jit(solution)/shard_map/weights/pallas_call | solution.py:280
  47.5 0.3 inner.15.refs_4_
  47.8 0.3 inner.16.refs_4_
  48.1 0.0 collective-permute-done.16.refs_0_
  48.1 0.6 inner.17
  48.7 20.3 %conditional.1 = (f32[8,8,128]{2,1,0:T(8,128)S(1)}, f32[1,6,2,2,128,128]{5,4,3,2,1,0:T(8,128)S(1)}, f32[1,6,2,2,128,128]{5,4,3,2,1,0:T(8,128)S(1)}, f32[1,8,128]{2,1,0:T(8,128)S(1)}) conditional(s32[]{:T(128)} %bitcast.2, (f32[4,6,2,2,128,128]{5,4,3,2,1,0:T(8,128)S(1)}, f32[4,6,2,2,128,128]{5,4,3,2,1,0:T(8,128)S(1)}, ...), branch_computations={%region_0.0_spmd, %region_1.0_spmd, %region_2.0_spmd, %region_3.0_... | conditional | flops 8000000 | bytes 17145840 | solution.py:498
  48.7 2.7 %collective-permute-start.1 = (bf16[2,3,2,128,128]{4,3,2,1,0:T(8,128)(2,1)S(1)}, bf16[2,3,2,128,128]{4,3,2,1,0:T(8,128)(2,1)S(1)}, u32[]{:S(2)}, u32[]{:S(2)}) collective-permute-start(bf16[2,3,2,128,128]{4,3,2,1,0:T(8,128)(2,1)S(1)} %get-tuple-element.60), channel_id=1, source_target_pairs={{8,0},{10,2},{4,12},{6,14},{24,16},{26,18},{20,28},{22,30}} | collective-permute-start | bytes 1179656 | tf_op jit(solution)/shard_map/cond/branch_1_fun/ppermute | solution.py:487
  51.4 1.3 %collective-permute-start = (bf16[2,3,2,128,128]{4,3,2,1,0:T(8,128)(2,1)S(1)}, bf16[2,3,2,128,128]{4,3,2,1,0:T(8,128)(2,1)S(1)}, u32[]{:S(2)}, u32[]{:S(2)}) collective-permute-start(bf16[2,3,2,128,128]{4,3,2,1,0:T(8,128)(2,1)S(1)} %get-tuple-element.56), channel_id=1, source_target_pairs={{8,0},{10,2},{4,12},{6,14},{24,16},{26,18},{20,28},{22,30}} | collective-permute-start | bytes 1179656 | tf_op jit(solution)/shard_map/cond/branch_1_fun/ppermute | solution.py:487
  52.8 0.4 stage.5
  53.1 11.3 %collective-permute-done.1.refs_0_ = bf16[2,3,2,128,128]{4,3,2,1,0:T(8,128)(2,1)S(1)} collective-permute-done((bf16[2,3,2,128,128]{4,3,2,1,0:T(8,128)(2,1)S(1)}, bf16[2,3,2,128,128]{4,3,2,1,0:T(8,128)(2,1)S(1)}, u32[]{:S(2)}, u32[]{:S(2)}) %collective-permute-start.1) | collective-permute-done | bytes 393248 | tf_op jit(solution)/shard_map/cond/branch_1_fun/ppermute | solution.py:487
  64.5 0.3 inner.9.refs_4_
  64.7 3.9 %collective-permute-done.refs_0_ = bf16[2,3,2,128,128]{4,3,2,1,0:T(8,128)(2,1)S(1)} collective-permute-done((bf16[2,3,2,128,128]{4,3,2,1,0:T(8,128)(2,1)S(1)}, bf16[2,3,2,128,128]{4,3,2,1,0:T(8,128)(2,1)S(1)}, u32[]{:S(2)}, u32[]{:S(2)}) %collective-permute-start) | collective-permute-done | bytes 393248 | tf_op jit(solution)/shard_map/cond/branch_1_fun/ppermute | solution.py:487
  68.7 0.3 inner.10
  69.0 0.0 collective-permute-done.9.field_ref
  69.0 0.6 last.1
  69.6 0.0 collective-permute-start.17
  69.6 1.1 %collective-permute-done.17 = f32[2,2,1]{2,1,0:T(2,128)S(1)} collective-permute-done((f32[2,2,1]{2,1,0:T(2,128)S(1)}, f32[2,2,1]{2,1,0:T(2,128)S(1)}, u32[]{:S(2)}, u32[]{:S(2)}) %collective-permute-start.17) | collective-permute-done | bytes 48 | tf_op jit(solution)/shard_map/ppermute | solution.py:418
  70.7 1.3 %collective-permute-start.18 = (f32[2,2,1]{2,1,0:T(2,128)S(1)}, f32[2,2,1]{2,1,0:T(2,128)S(1)}, u32[]{:S(2)}, u32[]{:S(2)}) collective-permute-start(f32[2,2,1]{2,1,0:T(2,128)S(1)} %add.6), channel_id=1, source_target_pairs={{0,8},{1,9},{2,10},{3,11},{12,4},{13,5},{14,6},{15,7},{16,24},{17,... | collective-permute-start | bytes 56 | tf_op jit(solution)/shard_map/ppermute | solution.py:503
  72.0 5.1 %collective-permute-done.18 = f32[2,2,1]{2,1,0:T(2,128)S(1)} collective-permute-done((f32[2,2,1]{2,1,0:T(2,128)S(1)}, f32[2,2,1]{2,1,0:T(2,128)S(1)}, u32[]{:S(2)}, u32[]{:S(2)}) %collective-permute-start.18) | collective-permute-done | bytes 48 | tf_op jit(solution)/shard_map/ppermute | solution.py:503
  77.1 0.7 copy.8
  (6 shorter events, 0.0 us)
Async XLA Ops:
  0.7 6.2 %copy-start.2 = (s32[1,4,6,2]{2,3,1,0:T(2,128)S(1)}, s32[1,4,6,2]{2,3,1,0:T(2,128)}, u32[]{:S(2)}) copy-start(s32[1,4,6,2]{2,3,1,0:T(2,128)} %param.10) | copy-start | bytes 580
  1.9 25.7 %collective-permute-start.7 = (bf16[2,3,2,128,128]{4,3,2,1,0:T(8,128)(2,1)S(1)}, bf16[2,3,2,128,128]{4,3,2,1,0:T(8,128)(2,1)S(1)}, u32[]{:S(2)}, u32[]{:S(2)}) collective-permute-start(bf16[2,3,2,128,128]{4,3,2,1,0:T(8,128)(2,1)S(1)} %get-tuple-element.108), channel_id=1, source_target_pairs={{8,0},{10,2},{4,12},{6,14},{9,1},{11,3},{5,13},{7,15},{24,16},{26,... | collective-permute-start | bytes 1179656 | tf_op jit(solution)/shard_map/ppermute | solution.py:419
  5.4 22.2 %collective-permute-start.8 = (bf16[2,3,2,128,128]{4,3,2,1,0:T(8,128)(2,1)S(1)}, bf16[2,3,2,128,128]{4,3,2,1,0:T(8,128)(2,1)S(1)}, u32[]{:S(2)}, u32[]{:S(2)}) collective-permute-start(bf16[2,3,2,128,128]{4,3,2,1,0:T(8,128)(2,1)S(1)} %get-tuple-element.109), channel_id=1, source_target_pairs={{8,0},{10,2},{4,12},{6,14},{9,1},{11,3},{5,13},{7,15},{24,16},{26,... | collective-permute-start | bytes 1179656 | tf_op jit(solution)/shard_map/ppermute | solution.py:419
  6.8 2.1 %collective-permute-start.6 = (s32[1]{0:T(128)}, s32[1]{0:T(128)}, u32[]{:S(2)}, u32[]{:S(2)}) collective-permute-start(s32[1]{0:T(128)} %param.11), channel_id=1, source_target_pairs={{0,1},{1,0},{2,3},{3,2},{4,5},{5,4},{6,7},{7,6},{8,9},{9,8},{10,11... | collective-permute-start | bytes 20 | tf_op jit(solution)/shard_map/ppermute | solution.py:418
  7.1 21.1 %collective-permute-start.12 = (s32[48]{0:T(128)S(1)}, s32[48]{0:T(128)S(1)}, u32[]{:S(2)}, u32[]{:S(2)}) collective-permute-start(s32[48]{0:T(128)S(1)} %reshape.10.refs_5_.refs_7_), channel_id=1, source_target_pairs={{0,1},{1,0},{2,3},{3,2},{4,5},{5,4},{6,7},{7,6},{8,9},{9,8},{10,11... | collective-permute-start | bytes 584 | tf_op jit(solution)/shard_map/ppermute | solution.py:418
  7.6 14.6 %collective-permute-start.10 = (s32[48]{0:T(128)S(1)}, s32[48]{0:T(128)S(1)}, u32[]{:S(2)}, u32[]{:S(2)}) collective-permute-start(s32[48]{0:T(128)S(1)} %reshape.10.refs_5_.refs_7_), channel_id=1, source_target_pairs={{8,0},{10,2},{4,12},{6,14},{9,1},{11,3},{5,13},{7,15},{24,16},{26,... | collective-permute-start | bytes 584 | tf_op jit(solution)/shard_map/ppermute | solution.py:419
  10.8 0.7 copy-start
  11.5 18.6 %copy-start.1 = (s32[8]{0:T(128)S(1)}, s32[8]{0:T(128)}, u32[]{:S(2)}) copy-start(s32[8]{0:T(128)} %get-tuple-element.112.refs_1_) | copy-start | bytes 100
  14.0 24.3 %collective-permute-start.15 = (bf16[2,6,2,128,128]{4,3,2,1,0:T(8,128)(2,1)S(1)}, bf16[2,6,2,128,128]{4,3,2,1,0:T(8,128)(2,1)S(1)}, u32[]{:S(2)}, u32[]{:S(2)}) collective-permute-start(bf16[2,6,2,128,128]{4,3,2,1,0:T(8,128)(2,1)S(1)} %get-tuple-element.115.refs_10_.refs_11_), channel_id=1, source_target_pairs={{0,1},{1,0},{2,3},{3,2},{4,5},{5,4},{6,7},{7,6},{8,9},{9,8},{10,11... | collective-permute-start | bytes 2359304 | tf_op jit(solution)/shard_map/ppermute | solution.py:418
  22.2 25.9 %collective-permute-start.16 = (bf16[2,6,2,128,128]{4,3,2,1,0:T(8,128)(2,1)S(1)}, bf16[2,6,2,128,128]{4,3,2,1,0:T(8,128)(2,1)S(1)}, u32[]{:S(2)}, u32[]{:S(2)}) collective-permute-start(bf16[2,6,2,128,128]{4,3,2,1,0:T(8,128)(2,1)S(1)} %get-tuple-element.116.refs_12_), channel_id=1, source_target_pairs={{8,0},{10,2},{4,12},{6,14},{9,1},{11,3},{5,13},{7,15},{24,16},{26,... | collective-permute-start | bytes 2359304 | tf_op jit(solution)/shard_map/ppermute | solution.py:419
  27.6 1.2 %collective-permute-start.11 = (s32[48]{0:T(128)S(1)}, s32[48]{0:T(128)S(1)}, u32[]{:S(2)}, u32[]{:S(2)}) collective-permute-start(s32[48]{0:T(128)S(1)} %collective-permute-done.10.refs_4_.refs_6_), channel_id=1, source_target_pairs={{0,1},{1,0},{2,3},{3,2},{4,5},{5,4},{6,7},{7,6},{8,9},{9,8},{10,11... | collective-permute-start | bytes 584 | tf_op jit(solution)/shard_map/ppermute | solution.py:418
  27.7 10.5 %collective-permute-start.13 = (bf16[2,3,2,128,128]{4,3,2,1,0:T(8,128)(2,1)S(1)}, bf16[2,3,2,128,128]{4,3,2,1,0:T(8,128)(2,1)S(1)}, u32[]{:S(2)}, u32[]{:S(2)}) collective-permute-start(bf16[2,3,2,128,128]{4,3,2,1,0:T(8,128)(2,1)S(1)} %collective-permute-done.7.refs_8_.refs_0_), channel_id=1, source_target_pairs={{0,1},{1,0},{2,3},{3,2},{4,5},{5,4},{6,7},{7,6},{8,9},{9,8},{10,11... | collective-permute-start | bytes 1179656 | tf_op jit(solution)/shard_map/ppermute | solution.py:418
  28.2 10.1 %collective-permute-start.14 = (bf16[2,3,2,128,128]{4,3,2,1,0:T(8,128)(2,1)S(1)}, bf16[2,3,2,128,128]{4,3,2,1,0:T(8,128)(2,1)S(1)}, u32[]{:S(2)}, u32[]{:S(2)}) collective-permute-start(bf16[2,3,2,128,128]{4,3,2,1,0:T(8,128)(2,1)S(1)} %collective-permute-done.8.refs_9_.refs_0_), channel_id=1, source_target_pairs={{0,1},{1,0},{2,3},{3,2},{4,5},{5,4},{6,7},{7,6},{8,9},{9,8},{10,11... | collective-permute-start | bytes 1179656 | tf_op jit(solution)/shard_map/ppermute | solution.py:418
  28.8 40.2 %collective-permute-start.9 = (bf16[2,6,2,128,128]{4,3,2,1,0:T(8,128)(2,1)S(1)}, bf16[2,6,2,128,128]{4,3,2,1,0:T(8,128)(2,1)S(1)}, u32[]{:S(2)}, u32[]{:S(2)}) collective-permute-start(bf16[2,6,2,128,128]{4,3,2,1,0:T(8,128)(2,1)S(1)} %get-tuple-element.110.refs_13_), channel_id=1, source_target_pairs={{8,0},{10,2},{4,12},{6,14},{9,1},{11,3},{5,13},{7,15},{24,16},{26,... | collective-permute-start | bytes 2359304 | tf_op jit(solution)/shard_map/ppermute | solution.py:419
  48.7 15.7 %collective-permute-start.1 = (bf16[2,3,2,128,128]{4,3,2,1,0:T(8,128)(2,1)S(1)}, bf16[2,3,2,128,128]{4,3,2,1,0:T(8,128)(2,1)S(1)}, u32[]{:S(2)}, u32[]{:S(2)}) collective-permute-start(bf16[2,3,2,128,128]{4,3,2,1,0:T(8,128)(2,1)S(1)} %get-tuple-element.60), channel_id=1, source_target_pairs={{8,0},{10,2},{4,12},{6,14},{24,16},{26,18},{20,28},{22,30}} | collective-permute-start | bytes 1179656 | tf_op jit(solution)/shard_map/cond/branch_1_fun/ppermute | solution.py:487
  51.4 17.2 %collective-permute-start = (bf16[2,3,2,128,128]{4,3,2,1,0:T(8,128)(2,1)S(1)}, bf16[2,3,2,128,128]{4,3,2,1,0:T(8,128)(2,1)S(1)}, u32[]{:S(2)}, u32[]{:S(2)}) collective-permute-start(bf16[2,3,2,128,128]{4,3,2,1,0:T(8,128)(2,1)S(1)} %get-tuple-element.56), channel_id=1, source_target_pairs={{8,0},{10,2},{4,12},{6,14},{24,16},{26,18},{20,28},{22,30}} | collective-permute-start | bytes 1179656 | tf_op jit(solution)/shard_map/cond/branch_1_fun/ppermute | solution.py:487
  69.6 1.2 %collective-permute-start.17 = (f32[2,2,1]{2,1,0:T(2,128)S(1)}, f32[2,2,1]{2,1,0:T(2,128)S(1)}, u32[]{:S(2)}, u32[]{:S(2)}) collective-permute-start(f32[2,2,1]{2,1,0:T(2,128)S(1)} %get-tuple-element.128), channel_id=1, source_target_pairs={{0,1},{1,0},{2,3},{3,2},{4,5},{5,4},{6,7},{7,6},{8,9},{9,8},{10,11... | collective-permute-start | bytes 56 | tf_op jit(solution)/shard_map/ppermute | solution.py:418
  70.7 6.4 %collective-permute-start.18 = (f32[2,2,1]{2,1,0:T(2,128)S(1)}, f32[2,2,1]{2,1,0:T(2,128)S(1)}, u32[]{:S(2)}, u32[]{:S(2)}) collective-permute-start(f32[2,2,1]{2,1,0:T(2,128)S(1)} %add.6), channel_id=1, source_target_pairs={{0,8},{1,9},{2,10},{3,11},{12,4},{13,5},{14,6},{15,7},{16,24},{17,... | collective-permute-start | bytes 56 | tf_op jit(solution)/shard_map/ppermute | solution.py:503
